TPU v7x, 512 devices: a whole 4x8x8 slice. The times are simulated.
512 devices in a mesh: replica: 64 (over x, y, z_lo), tensor: 8 (over z_hi, core).
Axes of the slice: x: 4, y: 8, z: 8 (z_hi: 4, z_lo: 2; z = z_hi * 2 + z_lo), core: 2. Of those that a mesh axis runs over, the one named last changes fastest.
Arguments:
- hidden_in: bfloat16 [3, 512, 8192], P(None, 'replica'), may hold values from -6 to 6
- frozen_query_rows: bfloat16 [3, 512, 8192], P(None, 'replica', 'tensor'), may hold values from -144 to 144
- base_key_value: bfloat16 [2, 3, 512, 1024], P(None, None, 'replica', 'tensor'), may hold values from -6 to 6
- cache: bfloat16 [2, 512, 384, 1024], P(None, 'replica', None, 'tensor'), may hold values from -6 to 6
- lengths: int32 [512], P('replica'), may hold values from 2 to 384, as said below
- switch_step: int32 [64], P('replica'), may hold values from 0 to 3
- old_down_q: bfloat16 [64, 8192], replicated, may hold values from -0.0625 to 0.0625
- current_query_up: bfloat16 [64, 8192], P(None, 'tensor'), may hold values from -0.75 to 0.75
- old_down_o: bfloat16 [64, 8192], P(None, 'tensor'), may hold values from -0.0625 to 0.0625
- old_up_o: bfloat16 [64, 8192], replicated, may hold values from -6 to 6
- new_down_q: bfloat16 [64, 8192], P('replica'), may hold values from -0.0625 to 0.0625
- refreshed_query_up: bfloat16 [64, 8192], P('replica', 'tensor'), may hold values from -0.75 to 0.75
- new_down_o: bfloat16 [64, 8192], P('replica', 'tensor'), may hold values from -0.0625 to 0.0625
- new_up_o: bfloat16 [64, 8192], P('replica'), may hold values from -6 to 6
Outputs:
- attended: bfloat16 [3, 512, 8192], P(None, 'replica', 'tensor')
- adapter_out: bfloat16 [3, 512, 8192], P(None, 'replica', 'tensor')
Inputs may be any that keep to these rules, and one draw needn't show every extreme that they name: `lengths`: the first sequence of every replica has all 384 positions live.
All inputs are finite; a program needn't handle non-finite values.
Results may differ from a plain program's by a relative error of at most 0.01.
Values may be sent and summed in bfloat16 or wider, within the bound.
A program may use at most 64 MiB of HBM per device.

v0:
```python
import jax
import jax.numpy as jnp
from jax import lax
from jax.sharding import PartitionSpec as P

HD = 128
STEPS = 3


def attend(query_matrix, cache_keys, cache_values, fresh_keys, fresh_values, lengths):
    score_scale = 1.0 / query_matrix.shape[-1] ** 0.5
    cache_scores = (
        jnp.einsum("bkgd,blkd->bkgl", query_matrix, cache_keys, preferred_element_type=jnp.float32)
        * score_scale
    )
    positions = jnp.arange(cache_keys.shape[1], dtype=jnp.int32)
    visible = (positions[None, :] < lengths[:, None])[:, None, None, :]
    cache_scores = jnp.where(visible, cache_scores, jnp.float32(-1e30))
    fresh_scores = (
        jnp.einsum("bkgd,bukd->bkgu", query_matrix, fresh_keys, preferred_element_type=jnp.float32)
        * score_scale
    )
    row_max = jnp.maximum(jnp.max(cache_scores, axis=-1), jnp.max(fresh_scores, axis=-1))[..., None]
    cache_exp = jnp.exp(cache_scores - row_max)
    fresh_exp = jnp.exp(fresh_scores - row_max)
    row_total = jnp.sum(cache_exp, axis=-1, keepdims=True) + jnp.sum(
        fresh_exp, axis=-1, keepdims=True
    )
    cache_weights = (cache_exp / row_total).astype(jnp.bfloat16)
    fresh_weights = (fresh_exp / row_total).astype(jnp.bfloat16)
    result = jnp.einsum(
        "bkgl,blkd->bkgd", cache_weights, cache_values, preferred_element_type=jnp.float32
    )
    result = result + jnp.einsum(
        "bkgu,bukd->bkgd", fresh_weights, fresh_values, preferred_element_type=jnp.float32
    )
    return result.astype(jnp.bfloat16)


def body(
    hidden_in,
    frozen_query_rows,
    base_key_value,
    cache,
    lengths,
    switch_step,
    old_down_q,
    current_query_up,
    old_down_o,
    old_up_o,
    new_down_q,
    refreshed_query_up,
    new_down_o,
    new_up_o,
):
    switch_at = switch_step[0]
    tensor_count = lax.axis_size("tensor")
    slice_width = new_down_q.shape[1] // tensor_count
    offset = lax.axis_index("tensor") * slice_width
    prior_up_o = lax.dynamic_slice_in_dim(old_up_o, offset, slice_width, 1)
    got_down_q, whole_up_o, got_up_q, got_down_o = (
        lax.all_gather(new_down_q, "replica", axis=0, tiled=True),
        lax.all_gather(new_up_o, "replica", axis=0, tiled=True),
        lax.all_gather(refreshed_query_up, "replica", axis=0, tiled=True),
        lax.all_gather(new_down_o, "replica", axis=0, tiled=True),
    )
    got_up_o = lax.dynamic_slice_in_dim(whole_up_o, offset, slice_width, 1)
    row_count = hidden_in.shape[1]
    cache_len = cache.shape[2]
    kv_local = base_key_value.shape[-1] // HD
    groups = frozen_query_rows.shape[-1] // base_key_value.shape[-1]
    cache_keys = cache[0].reshape(row_count, cache_len, kv_local, HD)
    cache_values = cache[1].reshape(row_count, cache_len, kv_local, HD)
    fresh_keys = jnp.transpose(base_key_value[0], (1, 0, 2)).reshape(row_count, STEPS, kv_local, HD)
    fresh_values = jnp.transpose(base_key_value[1], (1, 0, 2)).reshape(
        row_count, STEPS, kv_local, HD
    )
    attended_list = []
    adapter_list = []
    for decode_step in range(STEPS):
        adapter_swapped = decode_step >= switch_at
        query_up_weight = jnp.where(adapter_swapped, got_up_q, current_query_up)
        down_o = jnp.where(adapter_swapped, got_down_o, old_down_o)
        up_o = jnp.where(adapter_swapped, got_up_o, prior_up_o)
        down_q = jnp.where(adapter_swapped, got_down_q, old_down_q)
        rank_projected = jnp.dot(
            hidden_in[decode_step], down_q.T, preferred_element_type=jnp.float32
        ).astype(jnp.bfloat16)
        adapter_query_delta = jnp.dot(
            rank_projected, query_up_weight, preferred_element_type=jnp.float32
        )
        query_matrix = (
            frozen_query_rows[decode_step].astype(jnp.float32) + adapter_query_delta
        ).astype(jnp.bfloat16)
        query_matrix = query_matrix.reshape(row_count, kv_local, groups, HD)
        attended = attend(
            query_matrix,
            cache_keys,
            cache_values,
            fresh_keys[:, : decode_step + 1],
            fresh_values[:, : decode_step + 1],
            lengths,
        )
        attended = attended.reshape(row_count, kv_local * groups * HD)
        attended_list.append(attended)
        partial_value = jnp.dot(attended, down_o.T, preferred_element_type=jnp.float32)
        rank_sum = lax.psum(partial_value, "tensor").astype(jnp.bfloat16)
        adapter_list.append(
            jnp.dot(rank_sum, up_o, preferred_element_type=jnp.float32).astype(jnp.bfloat16)
        )
    return (jnp.stack(attended_list), jnp.stack(adapter_list))


def solution(mesh):
    placed = (
        P(None, "replica", None),
        P(None, "replica", "tensor"),
        P(None, None, "replica", "tensor"),
        P(None, "replica", None, "tensor"),
        P("replica"),
        P("replica"),
        P(),
        P(None, "tensor"),
        P(None, "tensor"),
        P(),
        P("replica", None),
        P("replica", "tensor"),
        P("replica", "tensor"),
        P("replica", None),
    )
    return jax.shard_map(
        body,
        mesh=mesh,
        in_specs=placed,
        out_specs=(P(None, "replica", "tensor"), P(None, "replica", "tensor")),
        check_vma=False,
    )
```

profile of v0, /device:TPU:8, one launch (start us, length us, event | category | flops | bytes accessed | tf_op | source)
XLA Modules:
  0.0 630.5 jit_solution(1585295844638863326)
XLA Ops:
  7.2 0.7 all-gather.7.cloned.1.call-update
  7.9 0.7 all-gather.9.cloned.1.call-update
  9.3 154.6 %all-gather.1 = bf16[64,1,1024]{2,1,0:T(2,128)(2,1)S(1)} all-gather(bf16[1,1,1024]{2,1,0:T(2,128)(2,1)} %bitcast.158), channel_id=1, replica_groups=mesh['replica'=64,'tensor'=8] {'replica'}, dimensions={0}, use_global_device_ids=true | all-gather | bytes 133120 | tf_op jit(solution)/shard_map/all_gather | solution.py:64
  163.9 0.7 iota_compare_fusion
  164.7 0.7 fusion.114
  165.4 151.8 %all-gather.2 = bf16[64,1,1024]{2,1,0:T(2,128)(2,1)S(1)} all-gather(bf16[1,1,1024]{2,1,0:T(2,128)(2,1)} %bitcast.159), channel_id=1, replica_groups=mesh['replica'=64,'tensor'=8] {'replica'}, dimensions={0}, use_global_device_ids=true | all-gather | bytes 133120 | tf_op jit(solution)/shard_map/all_gather | solution.py:65
  317.2 3.1 fusion.12
  320.5 0.5 fusion.115
  321.2 0.3 fusion.18
  321.5 0.2 fusion.8
  321.7 3.0 fusion.13
  324.7 0.5 fusion.117
  325.6 0.3 fusion.20
  325.9 3.0 fusion.14
  329.3 0.5 fusion.119
  329.9 0.3 fusion.4
  330.8 31.3 %all-reduce = (bf16[8,64]{1,0:T(8,128)(2,1)S(1)}, bf16[8,64]{1,0:T(8,128)(2,1)S(1)}, bf16[8,64]{1,0:T(8,128)(2,1)S(1)}) all-reduce(f32[8,64]{1,0:T(8,128)S(1)} %fusion.34, f32[8,64]{1,0:T(8,128)S(1)} %fusion.33, f32[8,64]{1,0:T(8,128)S(1)} %fusion.32), channel_id=1, replica_groups=mesh['replica'=64,'tensor'=8] {'tensor'}, use_global_device_ids=true, to_apply=%region_12.13 | all-reduce | flops 1536 | bytes 9216 | tf_op jit(solution)/shard_map/psum | solution.py:107
  362.1 255.9 %all-gather.9.cloned.1.call-done = bf16[64,1,8192]{2,1,0:T(2,128)(2,1)} async-done(((bf16[1,1,8192]{2,1,0:T(2,128)(2,1)}), bf16[64,1,8192]{2,1,0:T(2,128)(2,1)}) %all-gather.9.cloned.1.call-update) | async-done | bytes 1048592 | tf_op jit(solution)/shard_map/all_gather | solution.py:63
  618.0 1.2 constant_dynamic-slice_fusion
  619.2 1.1 fusion.11
  620.3 1.1 fusion.10
  621.4 1.1 fusion.9
  622.4 0.6 pad_maximum_fusion
  623.1 0.6 pad_maximum_fusion.1
  (37 shorter events, 1.9 us)
Async XLA Ops:
  7.2 310.0 %all-gather.7.cloned.1.call-start = ((), (), s32[]{:S(2)}) async-start(), calls=%async_computation | async-start | bytes 2129920 | tf_op jit(solution)/shard_map/all_gather | solution.py:62
  7.9 610.1 %all-gather.9.cloned.1.call-start = ((), (), s32[]{:S(2)}) async-start(), calls=%async_computation.1 | async-start | bytes 2129920 | tf_op jit(solution)/shard_map/all_gather | solution.py:63
  317.2 3.3 copy-start
  320.3 1.4 copy-start.1
  320.3 1.4 copy-start.2
  320.3 1.4 copy-start.4
  328.9 1.4 copy-start.3
Sparse Core Ops, SparseCore 0:
  10.1 306.4 all-gather.6
  318.6 299.3 all-gather.8
where the time goes:
time: 631 us
  blocking collectives  338 us (54%)
  waiting for transfers between devices  257 us (41%)
  matrix products  16 us (3%)
  between operations  14.9 us (2%)
    all_gather x1, waiting for transfers between devices, body(): lax.all_gather(new_up_o, 'replica', axis=0, tiled=True)  256 us
    all_gather x1, blocking collectives, body(): lax.all_gather(refreshed_query_up, 'replica', axis=0, tiled=True)  155 us
    all_gather x1, blocking collectives, body(): lax.all_gather(new_down_o, 'replica', axis=0, tiled=True)  152 us
    psum x1, blocking collectives, body(): rank_sum = lax.psum(partial_value, 'tensor').astype(jnp.bfloat16)  31.3 us
  transfers between devices with their start and end apart: 2, of which 1 were waited for; matrix products, arithmetic and copies ran while one was open for 2% of the time, Pallas kernels for 0%

commit v1 on v0

v1 whole, which is shorter than its diff:
```python
import functools

import jax
import jax.numpy as jnp
from jax import lax
from jax.experimental import pallas as pl
from jax.experimental.pallas import tpu as pltpu
from jax.sharding import PartitionSpec as P

HD = 128
STEPS = 3
ROWS = 8
RANK = 64
GROUP = 16
LANES = 128
MESH = pl.DeviceIdType.MESH
F32 = jnp.float32
BF16 = jnp.bfloat16


def nt(a, b):
    return lax.dot_general(a, b, (((1,), (1,)), ((), ())), preferred_element_type=F32)


def nn(a, b):
    return lax.dot_general(a, b, (((1,), (0,)), ((), ())), preferred_element_type=F32)


def kernel(
    n_block, n_tensor, width, cache_len, key_rows,
    lengths, switch, hidden, frozen, fresh, cache,
    old_dq, old_uq, old_do, old_uo, new_dq, new_uq, new_do, new_uo,
    attended_out, adapter_out,
    row_dq, row_uq, row_do, row_uo, hid, frz, frs, kbuf, vbuf,
    w_old, w_new, packs, landed, stage, spread, fresh_rows, q_heads, a_rows,
    part, parts, att_stage, ada_stage,
    loc, kv_sem, s1_send, s1_recv, s2_send, s2_recv, ar_send, ar_recv,
):
    replica = lax.axis_index("replica")
    tensor = lax.axis_index("tensor")
    mine = lax.rem(replica, GROUP)
    block = lax.div(replica, GROUP)
    base = block * GROUP
    cols = pl.ds(pl.multiple_of(tensor * width, width), width)
    heads = width // HD
    tiles = width // LANES

    local = [
        pltpu.make_async_copy(new_dq, row_dq, loc.at[0]),
        pltpu.make_async_copy(new_uq, row_uq, loc.at[1]),
        pltpu.make_async_copy(new_do, row_do, loc.at[2]),
        pltpu.make_async_copy(new_uo, row_uo, loc.at[3]),
        pltpu.make_async_copy(hidden.at[:, :, cols], hid, loc.at[4]),
        pltpu.make_async_copy(old_dq.at[:, cols], w_old.at[0], loc.at[5]),
        pltpu.make_async_copy(fresh, frs, loc.at[6]),
        pltpu.make_async_copy(old_uq, w_old.at[1], loc.at[7]),
        pltpu.make_async_copy(frozen, frz, loc.at[8]),
        pltpu.make_async_copy(old_do, w_old.at[2], loc.at[9]),
        pltpu.make_async_copy(old_uo.at[:, cols], w_old.at[3], loc.at[10]),
    ]
    for copy in local:
        copy.start()
    kv = []
    for b in range(ROWS):
        kv.append(pltpu.make_async_copy(cache.at[0, b], kbuf.at[b, pl.ds(0, cache_len)], kv_sem.at[0, b]))
        kv.append(pltpu.make_async_copy(cache.at[1, b], vbuf.at[b, pl.ds(0, cache_len)], kv_sem.at[1, b]))
    for copy in kv:
        copy.start()

    group_peers = [(base + lax.rem(mine + j, GROUP), tensor) for j in range(1, GROUP)]
    block_peers = [
        (lax.rem(block + j, n_block) * GROUP + mine, tensor) for j in range(1, n_block)
    ]
    tensor_peers = [(replica, lax.rem(tensor + j, n_tensor)) for j in range(1, n_tensor)]
    barrier = pltpu.get_barrier_semaphore()
    everyone = group_peers + block_peers + tensor_peers
    for peer in everyone:
        pl.semaphore_signal(barrier, inc=1, device_id=peer, device_id_type=MESH)

    for copy in local[:4]:
        copy.wait()
    for i, row in enumerate((row_dq[:, cols], row_uq[...], row_do[...], row_uo[:, cols])):
        row = row.astype(F32)
        for s in range(tiles):
            stage[i // 2, pl.ds((i % 2) * tiles + s, 1), :] = row[:, s * LANES : (s + 1) * LANES]
    for p in range(2):
        packs[p] = stage[p].astype(BF16)
        landed[p, mine] = packs[p]

    pl.semaphore_wait(barrier, len(everyone))

    for p in range(2):
        for peer in group_peers:
            pltpu.make_async_remote_copy(
                src_ref=packs.at[p],
                dst_ref=landed.at[p, mine],
                send_sem=s1_send.at[p],
                recv_sem=s1_recv.at[p],
                device_id=peer,
                device_id_type=MESH,
            ).start()

    local[6].wait()
    pad = key_rows - cache_len - 16
    for i, buf in enumerate((kbuf, vbuf)):
        for u in range(ROWS):
            if u < STEPS:
                fresh_rows[i, pl.ds(u * ROWS, ROWS), :] = frs[i, u].astype(F32)
            else:
                fresh_rows[i, pl.ds(u * ROWS, ROWS), :] = jnp.zeros((ROWS, HD), F32)
        for b in range(ROWS):
            rows = fresh_rows[i, pl.ds(b, ROWS, stride=ROWS), :]
            rows = jnp.concatenate([rows, jnp.zeros((8, HD), F32)], axis=0)
            buf[b, pl.ds(cache_len, 16), :] = rows.astype(BF16)
            buf[b, pl.ds(cache_len + 16, pad), :] = jnp.zeros((pad, HD), BF16)

    local[4].wait()
    hid_rows = jnp.concatenate([hid[t].astype(F32) for t in range(STEPS)], axis=0).astype(BF16)

    own_rows = pl.ds(pl.multiple_of(block * GROUP, GROUP), GROUP)

    def gathered(p):
        pltpu.make_async_copy(
            landed.at[p, pl.ds(0, GROUP - 1)], landed.at[p, pl.ds(0, GROUP - 1)], s1_recv.at[p]
        ).wait()
        spread[...] = landed[p].reshape(GROUP * 2 * tiles, LANES).astype(F32)
        for half in range(2):
            m = 2 * p + half
            for s in range(tiles):
                w_new[m, own_rows, s * LANES : (s + 1) * LANES] = spread[
                    pl.ds(half * tiles + s, GROUP, stride=2 * tiles), :
                ].astype(BF16)
            for peer in block_peers:
                pltpu.make_async_remote_copy(
                    src_ref=w_new.at[m, own_rows],
                    dst_ref=w_new.at[m, own_rows],
                    send_sem=s2_send.at[m],
                    recv_sem=s2_recv.at[m],
                    device_id=peer,
                    device_id_type=MESH,
                ).start()

    def weights(m):
        others = w_new.at[m, pl.ds(0, (n_block - 1) * GROUP)]
        pltpu.make_async_copy(others, others, s2_recv.at[m]).wait()
        return jnp.concatenate([w_old[m], w_new[m]], axis=0)

    lane_half = lax.div(lax.broadcasted_iota(jnp.int32, (ROWS, LANES), 1), RANK)
    switch_at = jnp.full((ROWS, LANES), switch[0], jnp.int32)
    half_of = [jnp.where(switch_at <= t, 1, 0) for t in range(STEPS)]

    def reduce_start(r, product):
        chosen = []
        for t in range(STEPS):
            rows = product[t * ROWS : (t + 1) * ROWS]
            chosen.append(jnp.where(half_of[t] == t % 2, rows, pltpu.roll(rows, RANK, 1)))
        tile = jnp.concatenate([jnp.where(lane_half == 0, chosen[0], chosen[1]), chosen[2]], axis=0)
        part[r] = tile
        parts[r, tensor] = tile
        for peer in tensor_peers:
            pltpu.make_async_remote_copy(
                src_ref=part.at[r],
                dst_ref=parts.at[r, tensor],
                send_sem=ar_send.at[r],
                recv_sem=ar_recv.at[r],
                device_id=peer,
                device_id_type=MESH,
            ).start()

    def reduce_done(r):
        others = parts.at[r, pl.ds(0, n_tensor - 1)]
        pltpu.make_async_copy(others, others, ar_recv.at[r]).wait()
        total = jnp.sum(parts[r], axis=0)
        rows = []
        for t in range(STEPS):
            tile = total[(t // 2) * ROWS : (t // 2 + 1) * ROWS]
            both = jnp.where(lane_half == t % 2, tile, pltpu.roll(tile, RANK, 1))
            rows.append(jnp.where(lane_half == half_of[t], both, 0.0))
        return jnp.concatenate(rows, axis=0).astype(BF16)

    gathered(0)
    gathered(1)

    local[5].wait()
    reduce_start(0, nt(hid_rows, weights(0)))

    local[7].wait()
    local[8].wait()
    up_q = weights(1)
    for copy in kv:
        copy.wait()
    low_rank = reduce_done(0)
    delta = nn(low_rank, up_q)
    for t in range(STEPS):
        for h in range(heads):
            at = slice(h * HD, (h + 1) * HD)
            q_heads[t, pl.ds(h * ROWS, ROWS), :] = (
                frz[t, :, at].astype(F32) + delta[t * ROWS : (t + 1) * ROWS, at]
            )

    scale = 1.0 / HD**0.5
    query_rows = STEPS * heads
    col = lax.broadcasted_iota(jnp.int32, (query_rows, key_rows), 1)
    row = lax.broadcasted_iota(jnp.int32, (query_rows, key_rows), 0)
    is_fresh = jnp.logical_and(col >= cache_len, (col - cache_len) * heads <= row)
    for b in range(ROWS):
        query = jnp.concatenate(
            [q_heads[t, pl.ds(b, heads, stride=ROWS), :] for t in range(STEPS)], axis=0
        ).astype(BF16)
        scores = nt(query, kbuf[b]) * scale
        live = jnp.logical_or(col < lengths[b], is_fresh)
        scores = jnp.where(live, scores, -1e30)
        top = jnp.max(scores, axis=1, keepdims=True)
        exps = jnp.exp(scores - top)
        total = jnp.sum(exps, axis=1, keepdims=True)
        probs = (exps * (1.0 / total)).astype(BF16)
        result = nn(probs, vbuf[b])
        for t in range(STEPS):
            a_rows[t, pl.ds(b * heads, heads), :] = result[t * heads : (t + 1) * heads]

    attended = []
    for t in range(STEPS):
        rows = jnp.concatenate(
            [a_rows[t, pl.ds(h, ROWS, stride=heads), :] for h in range(heads)], axis=1
        )
        attended.append(rows)
        att_stage[t] = rows.astype(BF16)
    att_copy = pltpu.make_async_copy(att_stage, attended_out, loc.at[11])
    att_copy.start()

    local[9].wait()
    reduce_start(1, nt(jnp.concatenate(attended, axis=0).astype(BF16), weights(2)))
    local[10].wait()
    up_o = weights(3)
    result = nn(reduce_done(1), up_o)
    for t in range(STEPS):
        ada_stage[t] = result[t * ROWS : (t + 1) * ROWS].astype(BF16)
    ada_copy = pltpu.make_async_copy(ada_stage, adapter_out, loc.at[12])
    ada_copy.start()

    for p in range(2):
        sent = landed.at[p, pl.ds(0, GROUP - 1)]
        pltpu.make_async_copy(sent, sent, s1_send.at[p]).wait()
    for m in range(4):
        sent = w_new.at[m, pl.ds(0, (n_block - 1) * GROUP)]
        pltpu.make_async_copy(sent, sent, s2_send.at[m]).wait()
    for r in range(2):
        sent = parts.at[r, pl.ds(0, n_tensor - 1)]
        pltpu.make_async_copy(sent, sent, ar_send.at[r]).wait()
    att_copy.wait()
    ada_copy.wait()


def body(
    n_replica, n_tensor,
    hidden_in, frozen_query_rows, base_key_value, cache, lengths, switch_step,
    old_down_q, current_query_up, old_down_o, old_up_o,
    new_down_q, refreshed_query_up, new_down_o, new_up_o,
):
    width = frozen_query_rows.shape[-1]
    cache_len = cache.shape[2]
    key_rows = cache_len + LANES
    tiles = width // LANES
    dma = pltpu.SemaphoreType.DMA
    out = jax.ShapeDtypeStruct(frozen_query_rows.shape, BF16)
    return pl.pallas_call(
        functools.partial(kernel, n_replica // GROUP, n_tensor, width, cache_len, key_rows),
        out_shape=(out, out),
        in_specs=[pl.BlockSpec(memory_space=pltpu.SMEM)] * 2
        + [pl.BlockSpec(memory_space=pl.ANY)] * 12,
        out_specs=(pl.BlockSpec(memory_space=pl.ANY),) * 2,
        scratch_shapes=[
            pltpu.VMEM(new_down_q.shape, BF16),
            pltpu.VMEM(refreshed_query_up.shape, BF16),
            pltpu.VMEM(new_down_o.shape, BF16),
            pltpu.VMEM(new_up_o.shape, BF16),
            pltpu.VMEM((STEPS, ROWS, width), BF16),
            pltpu.VMEM((STEPS, ROWS, width), BF16),
            pltpu.VMEM(base_key_value.shape, BF16),
            pltpu.VMEM((ROWS, key_rows, HD), BF16),
            pltpu.VMEM((ROWS, key_rows, HD), BF16),
            pltpu.VMEM((4, RANK, width), BF16),
            pltpu.VMEM((4, RANK, width), BF16),
            pltpu.VMEM((2, 2 * tiles, LANES), BF16),
            pltpu.VMEM((2, GROUP, 2 * tiles, LANES), BF16),
            pltpu.VMEM((2, 2 * tiles, LANES), F32),
            pltpu.VMEM((GROUP * 2 * tiles, LANES), F32),
            pltpu.VMEM((2, ROWS * ROWS, HD), F32),
            pltpu.VMEM((STEPS, width // HD * ROWS, HD), F32),
            pltpu.VMEM((STEPS, width // HD * ROWS, HD), F32),
            pltpu.VMEM((2, 2 * ROWS, LANES), F32),
            pltpu.VMEM((2, n_tensor, 2 * ROWS, LANES), F32),
            pltpu.VMEM((STEPS, ROWS, width), BF16),
            pltpu.VMEM((STEPS, ROWS, width), BF16),
            dma((13,)),
            dma((2, ROWS)),
            dma((2,)),
            dma((2,)),
            dma((4,)),
            dma((4,)),
            dma((2,)),
            dma((2,)),
        ],
        compiler_params=pltpu.CompilerParams(
            collective_id=0, has_side_effects=True, vmem_limit_bytes=32 * 1024 * 1024
        ),
    )(
        lengths, switch_step, hidden_in, frozen_query_rows, base_key_value, cache,
        old_down_q, current_query_up, old_down_o, old_up_o,
        new_down_q, refreshed_query_up, new_down_o, new_up_o,
    )


def solution(mesh):
    placed = (
        P(None, "replica", None),
        P(None, "replica", "tensor"),
        P(None, None, "replica", "tensor"),
        P(None, "replica", None, "tensor"),
        P("replica"),
        P("replica"),
        P(),
        P(None, "tensor"),
        P(None, "tensor"),
        P(),
        P("replica", None),
        P("replica", "tensor"),
        P("replica", "tensor"),
        P("replica", None),
    )
    return jax.shard_map(
        functools.partial(body, mesh.shape["replica"], mesh.shape["tensor"]),
        mesh=mesh,
        in_specs=placed,
        out_specs=(P(None, "replica", "tensor"), P(None, "replica", "tensor")),
        check_vma=False,
    )
```

time: 631 us -> 59 us (0.09)
  the two profiles are of different devices: /device:TPU:8 before, /device:TPU:1 now
where the time goes in v1:
time: 59 us; the launch traced here: 58.4 us
  Pallas kernels  44.1 us (75%)
  local copies, waits for them, and re-layouts  12.9 us (22%)
  between operations  1.31 us (2%)
    pallas_call x1, Pallas kernels, body(): pl.pallas_call(functools.partial(kernel, n_replica // GROUP, n_tensor, wi...  44.1 us
    unnamed x28, local copies, waits for them, and re-layouts  12.9 us

profile of v1, /device:TPU:1, one launch (start us, length us, event | category | flops | bytes accessed | tf_op | source)
XLA Modules:
  0.0 58.4 jit_solution(17275221910879587666)
XLA Ops:
  1.3 0.0 copy-start
  1.3 1.4 %copy-done = bf16[2,8,384,128]{3,2,1,0:T(8,128)(2,1)S(1)} copy-done((bf16[2,8,384,128]{3,2,1,0:T(8,128)(2,1)S(1)}, bf16[2,8,384,128]{3,2,1,0:T(8,128)(2,1)}, u32[]{:S(2)}) %copy-start) | copy-done | bytes 1572888
  2.7 0.0 copy-start.1
  2.7 1.2 %copy-done.1 = bf16[64,8192]{1,0:T(8,128)(2,1)S(1)} copy-done((bf16[64,8192]{1,0:T(8,128)(2,1)S(1)}, bf16[64,8192]{1,0:T(8,128)(2,1)}, u32[]{:S(2)}) %copy-start.1) | copy-done | bytes 1048600
  3.9 0.0 copy-start.2
  3.9 1.2 %copy-done.2 = bf16[64,8192]{1,0:T(8,128)(2,1)S(1)} copy-done((bf16[64,8192]{1,0:T(8,128)(2,1)S(1)}, bf16[64,8192]{1,0:T(8,128)(2,1)}, u32[]{:S(2)}) %copy-start.2) | copy-done | bytes 1048600
  5.1 0.0 copy-start.3
  5.1 1.0 %copy-done.3 = bf16[3,8,8192]{2,1,0:T(8,128)(2,1)S(1)} copy-done((bf16[3,8,8192]{2,1,0:T(8,128)(2,1)S(1)}, bf16[3,8,8192]{2,1,0:T(8,128)(2,1)}, u32[]{:S(2)}) %copy-start.3) | copy-done | bytes 393240
  6.1 0.0 copy-start.4
  6.1 0.9 %copy-done.4 = bf16[64,1024]{1,0:T(8,128)(2,1)S(1)} copy-done((bf16[64,1024]{1,0:T(8,128)(2,1)S(1)}, bf16[64,1024]{1,0:T(8,128)(2,1)}, u32[]{:S(2)}) %copy-start.4) | copy-done | bytes 131096
  7.0 0.0 copy-start.5
  7.0 0.9 %copy-done.5 = bf16[64,1024]{1,0:T(8,128)(2,1)S(1)} copy-done((bf16[64,1024]{1,0:T(8,128)(2,1)S(1)}, bf16[64,1024]{1,0:T(8,128)(2,1)}, u32[]{:S(2)}) %copy-start.5) | copy-done | bytes 131096
  7.9 0.0 copy-start.6
  7.9 0.8 %copy-done.6 = bf16[3,8,1024]{2,1,0:T(8,128)(2,1)S(1)} copy-done((bf16[3,8,1024]{2,1,0:T(8,128)(2,1)S(1)}, bf16[3,8,1024]{2,1,0:T(8,128)(2,1)}, u32[]{:S(2)}) %copy-start.6) | copy-done | bytes 49176
  8.7 0.0 copy-start.7
  8.7 0.8 %copy-done.7 = bf16[1,8192]{1,0:T(2,128)(2,1)S(1)} copy-done((bf16[1,8192]{1,0:T(2,128)(2,1)S(1)}, bf16[1,8192]{1,0:T(2,128)(2,1)}, u32[]{:S(2)}) %copy-start.7) | copy-done | bytes 16408
  9.5 0.8 %copy-done.8 = bf16[1,8192]{1,0:T(2,128)(2,1)S(1)} copy-done((bf16[1,8192]{1,0:T(2,128)(2,1)S(1)}, bf16[1,8192]{1,0:T(2,128)(2,1)}, u32[]{:S(2)}) %copy-start.8) | copy-done | bytes 16408
  10.3 0.7 %copy-done.9 = bf16[2,3,8,128]{3,2,1,0:T(8,128)(2,1)S(1)} copy-done((bf16[2,3,8,128]{3,2,1,0:T(8,128)(2,1)S(1)}, bf16[2,3,8,128]{3,2,1,0:T(8,128)(2,1)}, u32[]{:S(2)}) %copy-start.9) | copy-done | bytes 12312
  11.0 0.7 %copy-done.10 = bf16[1,1024]{1,0:T(2,128)(2,1)S(1)} copy-done((bf16[1,1024]{1,0:T(2,128)(2,1)S(1)}, bf16[1,1024]{1,0:T(2,128)(2,1)}, u32[]{:S(2)}) %copy-start.10) | copy-done | bytes 2072
  11.7 0.7 %copy-done.11 = bf16[1,1024]{1,0:T(2,128)(2,1)S(1)} copy-done((bf16[1,1024]{1,0:T(2,128)(2,1)S(1)}, bf16[1,1024]{1,0:T(2,128)(2,1)}, u32[]{:S(2)}) %copy-start.11) | copy-done | bytes 2072
  12.3 0.7 %copy-done.12 = s32[8]{0:T(128)S(1)} copy-done((s32[8]{0:T(128)S(1)}, s32[8]{0:T(128)}, u32[]{:S(2)}) %copy-start.12) | copy-done | bytes 56
  13.0 44.1 %shard_map.149 = (bf16[3,8,1024]{2,1,0:T(8,128)(2,1)S(1)}, bf16[3,8,1024]{2,1,0:T(8,128)(2,1)S(1)}) custom-call(s32[8]{0:T(128)S(1)} %copy-done.12, s32[1]{0:T(128)S(6)} %copy.18.switch, bf16[3,8,8192]{2,1,0:T(8,128)(2,1)S(1)} %copy-done.3, bf16[3,8,1024]{2,1,0:T(8,128)(2,1)S(1)} %copy-done.6, bf16[2,3,8,128]{3,2,1,0:T(8,128)(2,1)S(1)} %copy-done.9, ...), custom_call_target="tpu_custom_call" | custom-call | tf_op jit(solution)/shard_map/pallas_call | solution.py:266
  57.1 0.6 %copy.19 = bf16[3,8,1024]{2,1,0:T(8,128)(2,1)} copy(bf16[3,8,1024]{2,1,0:T(8,128)(2,1)S(1)} %get-tuple-element.4) | data formatting | bytes 98304
  57.8 0.6 %copy.20 = bf16[3,8,1024]{2,1,0:T(8,128)(2,1)} copy(bf16[3,8,1024]{2,1,0:T(8,128)(2,1)S(1)} %get-tuple-element.5) | data formatting | bytes 98304
  (5 shorter events, 0.0 us)
Async XLA Ops:
  1.3 1.4 %copy-start = (bf16[2,8,384,128]{3,2,1,0:T(8,128)(2,1)S(1)}, bf16[2,8,384,128]{3,2,1,0:T(8,128)(2,1)}, u32[]{:S(2)}) copy-start(bf16[2,8,384,128]{3,2,1,0:T(8,128)(2,1)} %cache.1) | copy-start | bytes 4718596
  2.7 1.2 %copy-start.1 = (bf16[64,8192]{1,0:T(8,128)(2,1)S(1)}, bf16[64,8192]{1,0:T(8,128)(2,1)}, u32[]{:S(2)}) copy-start(bf16[64,8192]{1,0:T(8,128)(2,1)} %old_dq.1) | copy-start | bytes 3145732
  3.9 1.2 %copy-start.2 = (bf16[64,8192]{1,0:T(8,128)(2,1)S(1)}, bf16[64,8192]{1,0:T(8,128)(2,1)}, u32[]{:S(2)}) copy-start(bf16[64,8192]{1,0:T(8,128)(2,1)} %old_uo.1) | copy-start | bytes 3145732
  5.1 1.0 %copy-start.3 = (bf16[3,8,8192]{2,1,0:T(8,128)(2,1)S(1)}, bf16[3,8,8192]{2,1,0:T(8,128)(2,1)}, u32[]{:S(2)}) copy-start(bf16[3,8,8192]{2,1,0:T(8,128)(2,1)} %hidden.1) | copy-start | bytes 1179652
  6.1 0.9 %copy-start.4 = (bf16[64,1024]{1,0:T(8,128)(2,1)S(1)}, bf16[64,1024]{1,0:T(8,128)(2,1)}, u32[]{:S(2)}) copy-start(bf16[64,1024]{1,0:T(8,128)(2,1)} %old_uq.1) | copy-start | bytes 393220
  7.0 0.9 %copy-start.5 = (bf16[64,1024]{1,0:T(8,128)(2,1)S(1)}, bf16[64,1024]{1,0:T(8,128)(2,1)}, u32[]{:S(2)}) copy-start(bf16[64,1024]{1,0:T(8,128)(2,1)} %old_do.1) | copy-start | bytes 393220
  7.9 0.8 %copy-start.6 = (bf16[3,8,1024]{2,1,0:T(8,128)(2,1)S(1)}, bf16[3,8,1024]{2,1,0:T(8,128)(2,1)}, u32[]{:S(2)}) copy-start(bf16[3,8,1024]{2,1,0:T(8,128)(2,1)} %frozen.1) | copy-start | bytes 147460
  8.7 0.8 %copy-start.7 = (bf16[1,8192]{1,0:T(2,128)(2,1)S(1)}, bf16[1,8192]{1,0:T(2,128)(2,1)}, u32[]{:S(2)}) copy-start(bf16[1,8192]{1,0:T(2,128)(2,1)} %new_dq.1) | copy-start | bytes 49156
  9.5 0.8 %copy-start.8 = (bf16[1,8192]{1,0:T(2,128)(2,1)S(1)}, bf16[1,8192]{1,0:T(2,128)(2,1)}, u32[]{:S(2)}) copy-start(bf16[1,8192]{1,0:T(2,128)(2,1)} %new_uo.1) | copy-start | bytes 49156
  10.3 0.7 %copy-start.9 = (bf16[2,3,8,128]{3,2,1,0:T(8,128)(2,1)S(1)}, bf16[2,3,8,128]{3,2,1,0:T(8,128)(2,1)}, u32[]{:S(2)}) copy-start(bf16[2,3,8,128]{3,2,1,0:T(8,128)(2,1)} %fresh.1) | copy-start | bytes 36868
  11.0 0.7 %copy-start.10 = (bf16[1,1024]{1,0:T(2,128)(2,1)S(1)}, bf16[1,1024]{1,0:T(2,128)(2,1)}, u32[]{:S(2)}) copy-start(bf16[1,1024]{1,0:T(2,128)(2,1)} %new_uq.1) | copy-start | bytes 6148
  11.7 0.7 %copy-start.11 = (bf16[1,1024]{1,0:T(2,128)(2,1)S(1)}, bf16[1,1024]{1,0:T(2,128)(2,1)}, u32[]{:S(2)}) copy-start(bf16[1,1024]{1,0:T(2,128)(2,1)} %new_do.1) | copy-start | bytes 6148
  12.3 0.7 %copy-start.12 = (s32[8]{0:T(128)S(1)}, s32[8]{0:T(128)}, u32[]{:S(2)}) copy-start(s32[8]{0:T(128)} %lengths.1) | copy-start | bytes 100

commit v2 on v1

--- a/solution.py
+++ b/solution.py
@@ -28,12 +28,12 @@
 
 def kernel(
     n_block, n_tensor, width, cache_len, key_rows,
-    lengths, switch, hidden, frozen, fresh, cache,
+    switch, lengths_in, hidden, frozen, fresh, cache,
     old_dq, old_uq, old_do, old_uo, new_dq, new_uq, new_do, new_uo,
     attended_out, adapter_out,
     row_dq, row_uq, row_do, row_uo, hid, frz, frs, kbuf, vbuf,
     w_old, w_new, packs, landed, stage, spread, fresh_rows, q_heads, a_rows,
-    part, parts, att_stage, ada_stage,
+    part, parts, att_stage, ada_stage, lengths,
     loc, kv_sem, s1_send, s1_recv, s2_send, s2_recv, ar_send, ar_recv,
 ):
     replica = lax.axis_index("replica")
@@ -57,6 +57,7 @@
         pltpu.make_async_copy(frozen, frz, loc.at[8]),
         pltpu.make_async_copy(old_do, w_old.at[2], loc.at[9]),
         pltpu.make_async_copy(old_uo.at[:, cols], w_old.at[3], loc.at[10]),
+        pltpu.make_async_copy(lengths_in, lengths, loc.at[13]),
     ]
     for copy in local:
         copy.start()
@@ -189,6 +190,7 @@
     up_q = weights(1)
     for copy in kv:
         copy.wait()
+    local[11].wait()
     low_rank = reduce_done(0)
     delta = nn(low_rank, up_q)
     for t in range(STEPS):
@@ -266,9 +268,9 @@
     return pl.pallas_call(
         functools.partial(kernel, n_replica // GROUP, n_tensor, width, cache_len, key_rows),
         out_shape=(out, out),
-        in_specs=[pl.BlockSpec(memory_space=pltpu.SMEM)] * 2
-        + [pl.BlockSpec(memory_space=pl.ANY)] * 12,
-        out_specs=(pl.BlockSpec(memory_space=pl.ANY),) * 2,
+        in_specs=[pl.BlockSpec(memory_space=pltpu.SMEM)]
+        + [pl.BlockSpec(memory_space=pltpu.HBM)] * 13,
+        out_specs=(pl.BlockSpec(memory_space=pltpu.HBM),) * 2,
         scratch_shapes=[
             pltpu.VMEM(new_down_q.shape, BF16),
             pltpu.VMEM(refreshed_query_up.shape, BF16),
@@ -292,7 +294,8 @@
             pltpu.VMEM((2, n_tensor, 2 * ROWS, LANES), F32),
             pltpu.VMEM((STEPS, ROWS, width), BF16),
             pltpu.VMEM((STEPS, ROWS, width), BF16),
-            dma((13,)),
+            pltpu.SMEM(lengths.shape, jnp.int32),
+            dma((14,)),
             dma((2, ROWS)),
             dma((2,)),
             dma((2,)),
@@ -302,10 +305,10 @@
             dma((2,)),
         ],
         compiler_params=pltpu.CompilerParams(
-            collective_id=0, has_side_effects=True, vmem_limit_bytes=32 * 1024 * 1024
+            collective_id=0, has_side_effects=True, vmem_limit_bytes=60 * 1024 * 1024
         ),
     )(
-        lengths, switch_step, hidden_in, frozen_query_rows, base_key_value, cache,
+        switch_step, lengths, hidden_in, frozen_query_rows, base_key_value, cache,
         old_down_q, current_query_up, old_down_o, old_up_o,
         new_down_q, refreshed_query_up, new_down_o, new_up_o,
     )

time: 59 us -> 45.9 us (0.78)
  local copies, waits for them, and re-layouts: 12.9 us -> 2.84 us
  Pallas kernels: 44.1 us -> 41.5 us
    unnamed x28 -> x2, local copies, waits for them, and re-layouts: 12.9 us -> 2.84 us
    pallas_call x1, Pallas kernels: 44.1 us -> 41.5 us  [body(): pl.pallas_call(functools.partial(kernel, n_replica // GROUP, n_tensor, wi...]
where the time goes in v2:
time: 45.9 us; the launch traced here: 45.7 us
  Pallas kernels  41.5 us (90%)
  local copies, waits for them, and re-layouts  2.84 us (6%)
  between operations  1.29 us (3%)
    pallas_call x1, Pallas kernels, body(): pl.pallas_call(functools.partial(kernel, n_replica // GROUP, n_tensor, wi...  41.5 us
    unnamed x2, local copies, waits for them, and re-layouts  2.84 us

profile of v2, /device:TPU:1, one launch (start us, length us, event | category | flops | bytes accessed | tf_op | source)
XLA Modules:
  0.0 45.7 jit_solution(795637924595245818)
XLA Ops:
  1.3 41.5 %shard_map.149 = (bf16[3,8,1024]{2,1,0:T(8,128)(2,1)}, bf16[3,8,1024]{2,1,0:T(8,128)(2,1)}) custom-call(s32[1]{0:T(128)S(6)} %copy.18.switch, s32[8]{0:T(128)} %lengths_in.1, bf16[3,8,8192]{2,1,0:T(8,128)(2,1)} %hidden.1, bf16[3,8,1024]{2,1,0:T(8,128)(2,1)} %frozen.1, bf16[2,3,8,128]{3,2,1,0:T(8,128)(2,1)} %fresh.1, bf16[2,8,384,128]{3,2,1,0:T(8,128)(2,1)} %cache.1, ...), custom_call_target="tpu_custom_call" | custom-call | tf_op jit(solution)/shard_map/pallas_call | solution.py:268
  42.8 1.4 %copy.19 = bf16[3,8,1024]{2,1,0:T(8,128)(2,1)} copy(bf16[3,8,1024]{2,1,0:T(8,128)(2,1)} %get-tuple-element.4) | data formatting | bytes 98304
  44.2 1.4 %copy.20 = bf16[3,8,1024]{2,1,0:T(8,128)(2,1)} copy(bf16[3,8,1024]{2,1,0:T(8,128)(2,1)} %get-tuple-element.5) | data formatting | bytes 98304

commit v3 on v2

--- a/solution.py
+++ b/solution.py
@@ -33,7 +33,7 @@
     attended_out, adapter_out,
     row_dq, row_uq, row_do, row_uo, hid, frz, frs, kbuf, vbuf,
     w_old, w_new, packs, landed, stage, spread, fresh_rows, q_heads, a_rows,
-    part, parts, att_stage, ada_stage, lengths,
+    part, parts, lengths,
     loc, kv_sem, s1_send, s1_recv, s2_send, s2_recv, ar_send, ar_recv,
 ):
     replica = lax.axis_index("replica")
@@ -44,6 +44,19 @@
     cols = pl.ds(pl.multiple_of(tensor * width, width), width)
     heads = width // HD
     tiles = width // LANES
+
+    group_peers = [
+        (base + lax.rem(mine + GROUP // 2 + j, GROUP), tensor)
+        for j in sorted(range(1 - GROUP // 2, GROUP // 2), key=abs)
+    ]
+    block_peers = [
+        (lax.rem(block + j, n_block) * GROUP + mine, tensor) for j in (2, 1, 3)
+    ]
+    tensor_peers = [(replica, lax.rem(tensor + j, n_tensor)) for j in (4, 3, 5, 2, 6, 1, 7)]
+    barrier = pltpu.get_barrier_semaphore()
+    everyone = group_peers + block_peers + tensor_peers
+    for peer in everyone:
+        pl.semaphore_signal(barrier, inc=1, device_id=peer, device_id_type=MESH)
 
     local = [
         pltpu.make_async_copy(new_dq, row_dq, loc.at[0]),
@@ -57,26 +70,14 @@
         pltpu.make_async_copy(frozen, frz, loc.at[8]),
         pltpu.make_async_copy(old_do, w_old.at[2], loc.at[9]),
         pltpu.make_async_copy(old_uo.at[:, cols], w_old.at[3], loc.at[10]),
-        pltpu.make_async_copy(lengths_in, lengths, loc.at[13]),
+        pltpu.make_async_copy(lengths_in, lengths, loc.at[11]),
     ]
-    for copy in local:
+    for copy in local[:5]:
         copy.start()
     kv = []
     for b in range(ROWS):
         kv.append(pltpu.make_async_copy(cache.at[0, b], kbuf.at[b, pl.ds(0, cache_len)], kv_sem.at[0, b]))
         kv.append(pltpu.make_async_copy(cache.at[1, b], vbuf.at[b, pl.ds(0, cache_len)], kv_sem.at[1, b]))
-    for copy in kv:
-        copy.start()
-
-    group_peers = [(base + lax.rem(mine + j, GROUP), tensor) for j in range(1, GROUP)]
-    block_peers = [
-        (lax.rem(block + j, n_block) * GROUP + mine, tensor) for j in range(1, n_block)
-    ]
-    tensor_peers = [(replica, lax.rem(tensor + j, n_tensor)) for j in range(1, n_tensor)]
-    barrier = pltpu.get_barrier_semaphore()
-    everyone = group_peers + block_peers + tensor_peers
-    for peer in everyone:
-        pl.semaphore_signal(barrier, inc=1, device_id=peer, device_id_type=MESH)
 
     for copy in local[:4]:
         copy.wait()
@@ -100,6 +101,9 @@
                 device_id=peer,
                 device_id_type=MESH,
             ).start()
+
+    for copy in local[5:] + kv:
+        copy.start()
 
     local[6].wait()
     pad = key_rows - cache_len - 16
@@ -226,9 +230,7 @@
             [a_rows[t, pl.ds(h, ROWS, stride=heads), :] for h in range(heads)], axis=1
         )
         attended.append(rows)
-        att_stage[t] = rows.astype(BF16)
-    att_copy = pltpu.make_async_copy(att_stage, attended_out, loc.at[11])
-    att_copy.start()
+        attended_out[t] = rows.astype(BF16)
 
     local[9].wait()
     reduce_start(1, nt(jnp.concatenate(attended, axis=0).astype(BF16), weights(2)))
@@ -236,9 +238,7 @@
     up_o = weights(3)
     result = nn(reduce_done(1), up_o)
     for t in range(STEPS):
-        ada_stage[t] = result[t * ROWS : (t + 1) * ROWS].astype(BF16)
-    ada_copy = pltpu.make_async_copy(ada_stage, adapter_out, loc.at[12])
-    ada_copy.start()
+        adapter_out[t] = result[t * ROWS : (t + 1) * ROWS].astype(BF16)
 
     for p in range(2):
         sent = landed.at[p, pl.ds(0, GROUP - 1)]
@@ -249,8 +249,6 @@
     for r in range(2):
         sent = parts.at[r, pl.ds(0, n_tensor - 1)]
         pltpu.make_async_copy(sent, sent, ar_send.at[r]).wait()
-    att_copy.wait()
-    ada_copy.wait()
 
 
 def body(
@@ -264,13 +262,13 @@
     key_rows = cache_len + LANES
     tiles = width // LANES
     dma = pltpu.SemaphoreType.DMA
-    out = jax.ShapeDtypeStruct(frozen_query_rows.shape, BF16)
+    out = pltpu.VMEM(frozen_query_rows.shape, BF16)
     return pl.pallas_call(
         functools.partial(kernel, n_replica // GROUP, n_tensor, width, cache_len, key_rows),
         out_shape=(out, out),
         in_specs=[pl.BlockSpec(memory_space=pltpu.SMEM)]
         + [pl.BlockSpec(memory_space=pltpu.HBM)] * 13,
-        out_specs=(pl.BlockSpec(memory_space=pltpu.HBM),) * 2,
+        out_specs=(pl.BlockSpec(memory_space=pltpu.VMEM),) * 2,
         scratch_shapes=[
             pltpu.VMEM(new_down_q.shape, BF16),
             pltpu.VMEM(refreshed_query_up.shape, BF16),
@@ -292,10 +290,8 @@
             pltpu.VMEM((STEPS, width // HD * ROWS, HD), F32),
             pltpu.VMEM((2, 2 * ROWS, LANES), F32),
             pltpu.VMEM((2, n_tensor, 2 * ROWS, LANES), F32),
-            pltpu.VMEM((STEPS, ROWS, width), BF16),
-            pltpu.VMEM((STEPS, ROWS, width), BF16),
             pltpu.SMEM(lengths.shape, jnp.int32),
-            dma((14,)),
+            dma((12,)),
             dma((2, ROWS)),
             dma((2,)),
             dma((2,)),
@@ -305,12 +301,18 @@
             dma((2,)),
         ],
         compiler_params=pltpu.CompilerParams(
-            collective_id=0, has_side_effects=True, vmem_limit_bytes=60 * 1024 * 1024
+            collective_id=0, has_side_effects=True, vmem_limit_bytes=32 * 1024 * 1024
         ),
     )(
-        switch_step, lengths, hidden_in, frozen_query_rows, base_key_value, cache,
-        old_down_q, current_query_up, old_down_o, old_up_o,
-        new_down_q, refreshed_query_up, new_down_o, new_up_o,
+        switch_step,
+        *[
+            pltpu.with_memory_space_constraint(operand, pltpu.HBM)
+            for operand in (
+                lengths, hidden_in, frozen_query_rows, base_key_value, cache,
+                old_down_q, current_query_up, old_down_o, old_up_o,
+                new_down_q, refreshed_query_up, new_down_o, new_up_o,
+            )
+        ],
     )
 
 

time: 45.9 us -> 42.4 us (0.924)
  Pallas kernels: 41.5 us -> 39.6 us
  local copies, waits for them, and re-layouts: 2.84 us -> 1.24 us
    pallas_call x1, Pallas kernels: 41.5 us -> 39.6 us  [body(): pl.pallas_call(functools.partial(kernel, n_replica // GROUP, n_tensor, wi...]
    unnamed x2, local copies, waits for them, and re-layouts: 2.84 us -> 1.24 us
where the time goes in v3:
time: 42.4 us; the launch traced here: 42.2 us
  Pallas kernels  39.6 us (93%)
  between operations  1.29 us (3%)
  local copies, waits for them, and re-layouts  1.24 us (3%)
    pallas_call x1, Pallas kernels, body(): pl.pallas_call(functools.partial(kernel, n_replica // GROUP, n_tensor, wi...  39.6 us
    unnamed x2, local copies, waits for them, and re-layouts  1.24 us

profile of v3, /device:TPU:1, one launch (start us, length us, event | category | flops | bytes accessed | tf_op | source)
XLA Modules:
  0.0 42.2 jit_solution(3904360740664640597)
XLA Ops:
  1.3 39.6 %shard_map.149 = (bf16[3,8,1024]{2,1,0:T(8,128)(2,1)S(1)}, bf16[3,8,1024]{2,1,0:T(8,128)(2,1)S(1)}) custom-call(s32[1]{0:T(128)S(6)} %copy.20.switch, s32[8]{0:T(128)} %lengths_in.1, bf16[3,8,8192]{2,1,0:T(8,128)(2,1)} %hidden.1, bf16[3,8,1024]{2,1,0:T(8,128)(2,1)} %frozen.1, bf16[2,3,8,128]{3,2,1,0:T(8,128)(2,1)} %fresh.1, bf16[2,8,384,128]{3,2,1,0:T(8,128)(2,1)} %cache.1, ...), custom_call_target="tpu_custom_call" | custom-call | tf_op jit(solution)/shard_map/pallas_call | solution.py:266
  40.9 0.6 %copy.18 = bf16[3,8,1024]{2,1,0:T(8,128)(2,1)} copy(bf16[3,8,1024]{2,1,0:T(8,128)(2,1)S(1)} %get-tuple-element.2) | data formatting | bytes 98304
  41.6 0.6 %copy.19 = bf16[3,8,1024]{2,1,0:T(8,128)(2,1)} copy(bf16[3,8,1024]{2,1,0:T(8,128)(2,1)S(1)} %get-tuple-element.3) | data formatting | bytes 98304

commit v4 on v3

v4 whole, which is shorter than its diff:
```python
import functools

import jax
import jax.numpy as jnp
from jax import lax
from jax.experimental import pallas as pl
from jax.experimental.pallas import tpu as pltpu
from jax.sharding import PartitionSpec as P

HD = 128
STEPS = 3
ROWS = 8
RANK = 64
GROUP = 16
LANES = 128
MESH = pl.DeviceIdType.MESH
F32 = jnp.float32
BF16 = jnp.bfloat16


def nt(a, b):
    return lax.dot_general(a, b, (((1,), (1,)), ((), ())), preferred_element_type=F32)


def nn(a, b):
    return lax.dot_general(a, b, (((1,), (0,)), ((), ())), preferred_element_type=F32)


def kernel(
    n_block, n_tensor, width, cache_len, key_rows,
    switch, lengths_in, hidden, frozen, fresh, cache,
    old_dq, old_uq, old_do, old_uo, new_dq, new_uq, new_do, new_uo,
    attended_out, adapter_out,
    row_dq, row_uq, row_do, row_uo, hid_own, hid_rows, hid_full, dq_full, frz, frs, kbuf, vbuf,
    w_old, w_new, packs, landed, stage, spread, fresh_rows, old_rank, q_heads, a_rows,
    rank_part, rank_parts, part, parts, lengths,
    loc, kv_sem, s1_send, s1_recv, hid_send, hid_recv, s2_send, s2_recv,
    rank_send, rank_recv, sum_send, sum_recv,
):
    replica = lax.axis_index("replica")
    tensor = lax.axis_index("tensor")
    mine = lax.rem(replica, GROUP)
    block = lax.div(replica, GROUP)
    base = block * GROUP
    cols = pl.ds(pl.multiple_of(tensor * width, width), width)
    heads = width // HD
    tiles = width // LANES

    def block_at(j):
        return lax.rem(block + j, n_block)

    def tensor_at(j):
        return lax.rem(tensor + j, n_tensor)

    block_order = sorted(range(n_block), key=lambda j: -min(j, n_block - j))
    tensor_order = sorted(range(n_tensor), key=lambda j: -min(j, n_tensor - j))
    group_peers = [
        (base + lax.rem(mine + GROUP // 2 + j, GROUP), tensor)
        for j in sorted(range(1 - GROUP // 2, GROUP // 2), key=abs)
    ]
    block_peers = [(block_at(j) * GROUP + mine, tensor) for j in block_order if j]
    tensor_peers = [(replica, tensor_at(j)) for j in tensor_order if j]
    rank_peers = [
        (block_at(i), (block_at(i) * GROUP + mine, tensor_at(j)))
        for i in block_order
        for j in tensor_order
        if i or j
    ]
    barrier = pltpu.get_barrier_semaphore()
    everyone = group_peers + [peer for _, peer in rank_peers]
    for peer in everyone:
        pl.semaphore_signal(barrier, inc=1, device_id=peer, device_id_type=MESH)

    def send(src, dst, send_sem, recv_sem, peer):
        pltpu.make_async_remote_copy(
            src_ref=src,
            dst_ref=dst,
            send_sem=send_sem,
            recv_sem=recv_sem,
            device_id=peer,
            device_id_type=MESH,
        ).start()

    def wait_bytes(ref, sem):
        pltpu.make_async_copy(ref, ref, sem).wait()

    local = [
        pltpu.make_async_copy(new_dq, row_dq, loc.at[0]),
        pltpu.make_async_copy(new_uq, row_uq, loc.at[1]),
        pltpu.make_async_copy(new_do, row_do, loc.at[2]),
        pltpu.make_async_copy(new_uo, row_uo, loc.at[3]),
        pltpu.make_async_copy(hidden.at[:, :, cols], hid_own.at[block], loc.at[4]),
        pltpu.make_async_copy(fresh, frs, loc.at[5]),
        pltpu.make_async_copy(hidden, hid_full, loc.at[6]),
        pltpu.make_async_copy(old_dq, dq_full, loc.at[7]),
        pltpu.make_async_copy(old_uq, w_old.at[0], loc.at[8]),
        pltpu.make_async_copy(frozen, frz, loc.at[9]),
        pltpu.make_async_copy(old_do, w_old.at[1], loc.at[10]),
        pltpu.make_async_copy(old_uo.at[:, cols], w_old.at[2], loc.at[11]),
        pltpu.make_async_copy(lengths_in, lengths, loc.at[12]),
    ]
    for copy in local[:5]:
        copy.start()
    kv = []
    for b in range(ROWS):
        kv.append(pltpu.make_async_copy(cache.at[0, b], kbuf.at[b, pl.ds(0, cache_len)], kv_sem.at[0, b]))
        kv.append(pltpu.make_async_copy(cache.at[1, b], vbuf.at[b, pl.ds(0, cache_len)], kv_sem.at[1, b]))

    for copy in local[:4]:
        copy.wait()
    for i, row in enumerate((row_dq[:, cols], row_uq[...], row_do[...], row_uo[:, cols])):
        row = row.astype(F32)
        for s in range(tiles):
            stage[i // 2, pl.ds((i % 2) * tiles + s, 1), :] = row[:, s * LANES : (s + 1) * LANES]
    for p in range(2):
        packs[p] = stage[p].astype(BF16)
        landed[p, mine] = packs[p]

    pl.semaphore_wait(barrier, len(everyone))

    for peer in group_peers:
        send(packs.at[0], landed.at[0, mine], s1_send.at[0], s1_recv.at[0], peer)
    local[4].wait()
    for peer in block_peers:
        send(hid_own.at[block], hid_own.at[block], hid_send, hid_recv, peer)
    for peer in group_peers:
        send(packs.at[1], landed.at[1, mine], s1_send.at[1], s1_recv.at[1], peer)

    for copy in local[5:] + kv:
        copy.start()

    local[5].wait()
    pad = key_rows - cache_len - 16
    for i, buf in enumerate((kbuf, vbuf)):
        for u in range(ROWS):
            if u < STEPS:
                fresh_rows[i, pl.ds(u * ROWS, ROWS), :] = frs[i, u].astype(F32)
            else:
                fresh_rows[i, pl.ds(u * ROWS, ROWS), :] = jnp.zeros((ROWS, HD), F32)
        for b in range(ROWS):
            rows = fresh_rows[i, pl.ds(b, ROWS, stride=ROWS), :]
            rows = jnp.concatenate([rows, jnp.zeros((8, HD), F32)], axis=0)
            buf[b, pl.ds(cache_len, 16), :] = rows.astype(BF16)
            buf[b, pl.ds(cache_len + 16, pad), :] = jnp.zeros((pad, HD), BF16)

    wait_bytes(hid_own.at[pl.ds(0, n_block - 1)], hid_recv)
    for k in range(n_block):
        rows = jnp.concatenate([hid_own[k, t].astype(F32) for t in range(STEPS)], axis=0)
        hid_rows[pl.ds(k * STEPS * ROWS, STEPS * ROWS), :] = rows.astype(BF16)

    own_rows = pl.ds(pl.multiple_of(block * GROUP, GROUP), GROUP)
    lane = lax.broadcasted_iota(jnp.int32, (ROWS, LANES), 1)
    lane_half = lax.div(lane, RANK)
    lane_group = lax.div(lane, GROUP)

    def arrived(p):
        wait_bytes(landed.at[p, pl.ds(0, GROUP - 1)], s1_recv.at[p])
        spread[p] = landed[p].reshape(GROUP * 2 * tiles, LANES).astype(F32)

    def rows_of(i):
        return [
            spread[i // 2, pl.ds((i % 2) * tiles + s, GROUP, stride=2 * tiles), :].astype(BF16)
            for s in range(tiles)
        ]

    def share(m):
        for s, tile in enumerate(rows_of(m + 1)):
            w_new[m, own_rows, s * LANES : (s + 1) * LANES] = tile
        for peer in block_peers:
            send(w_new.at[m, own_rows], w_new.at[m, own_rows], s2_send.at[m], s2_recv.at[m], peer)

    def weights(m):
        wait_bytes(w_new.at[m, pl.ds(0, (n_block - 1) * GROUP)], s2_recv.at[m])
        return jnp.concatenate([w_old[m], w_new[m]], axis=0)

    arrived(0)
    down_q = jnp.concatenate(rows_of(0), axis=1)
    ranks = nt(hid_rows[...], jnp.concatenate([down_q] * (LANES // GROUP), axis=0))
    for k in range(n_block):
        tile = jnp.zeros((ROWS, LANES), F32)
        for t in range(STEPS):
            at = (k * STEPS + t) * ROWS
            tile = jnp.where(lane_group == t, ranks[at : at + ROWS], tile)
        rank_part[k] = tile
    slot = block * n_tensor + tensor
    rank_parts[slot] = rank_part[block]
    for k, peer in rank_peers:
        send(rank_part.at[k], rank_parts.at[slot], rank_send, rank_recv, peer)

    share(0)
    arrived(1)
    share(1)
    share(2)

    local[6].wait()
    local[7].wait()
    old_rank[...] = jnp.zeros_like(old_rank)
    old = jnp.zeros((STEPS * ROWS, RANK), F32)
    for c in range(n_tensor):
        at = slice(c * width, (c + 1) * width)
        rows = jnp.concatenate([hid_full[t, :, at].astype(F32) for t in range(STEPS)], axis=0)
        old = old + nt(rows.astype(BF16), dq_full[:, at])
    old_rank[:, 0:RANK] = old

    switch_at = jnp.full((ROWS, LANES), switch[0], jnp.int32)
    half_of = [jnp.where(switch_at <= t, 1, 0) for t in range(STEPS)]

    for i in (8, 9, 10, 11, 12):
        local[i].wait()
    for copy in kv:
        copy.wait()

    wait_bytes(rank_parts.at[pl.ds(0, n_block * n_tensor - 1)], rank_recv)
    sums = [
        jnp.sum(rank_parts[k * n_tensor : (k + 1) * n_tensor], axis=0) for k in range(n_block)
    ]
    chosen = []
    for t in range(STEPS):
        both = old_rank[t * ROWS : (t + 1) * ROWS]
        for k in range(n_block):
            at = RANK // GROUP + k
            moved = pltpu.roll(sums[k], (at - t) * GROUP, 1)
            both = jnp.where(lane_group == at, moved, both)
        chosen.append(jnp.where(lane_half == half_of[t], both, 0.0))
    low_rank = jnp.concatenate(chosen, axis=0).astype(BF16)
    delta = nn(low_rank, weights(0))
    for t in range(STEPS):
        for h in range(heads):
            at = slice(h * HD, (h + 1) * HD)
            q_heads[t, pl.ds(h * ROWS, ROWS), :] = (
                frz[t, :, at].astype(F32) + delta[t * ROWS : (t + 1) * ROWS, at]
            )

    scale = 1.0 / HD**0.5
    query_rows = STEPS * heads
    col = lax.broadcasted_iota(jnp.int32, (query_rows, key_rows), 1)
    row = lax.broadcasted_iota(jnp.int32, (query_rows, key_rows), 0)
    is_fresh = jnp.logical_and(col >= cache_len, (col - cache_len) * heads <= row)
    for b in range(ROWS):
        query = jnp.concatenate(
            [q_heads[t, pl.ds(b, heads, stride=ROWS), :] for t in range(STEPS)], axis=0
        ).astype(BF16)
        scores = nt(query, kbuf[b]) * scale
        live = jnp.logical_or(col < lengths[b], is_fresh)
        scores = jnp.where(live, scores, -1e30)
        top = jnp.max(scores, axis=1, keepdims=True)
        exps = jnp.exp(scores - top)
        total = jnp.sum(exps, axis=1, keepdims=True)
        probs = (exps * (1.0 / total)).astype(BF16)
        result = nn(probs, vbuf[b])
        for t in range(STEPS):
            a_rows[t, pl.ds(b * heads, heads), :] = result[t * heads : (t + 1) * heads]

    attended = []
    for t in range(STEPS):
        rows = jnp.concatenate(
            [a_rows[t, pl.ds(h, ROWS, stride=heads), :] for h in range(heads)], axis=1
        )
        attended.append(rows)
        attended_out[t] = rows.astype(BF16)

    product = nt(jnp.concatenate(attended, axis=0).astype(BF16), weights(1))
    picked = []
    for t in range(STEPS):
        rows = product[t * ROWS : (t + 1) * ROWS]
        picked.append(jnp.where(half_of[t] == t % 2, rows, pltpu.roll(rows, RANK, 1)))
    tile = jnp.concatenate([jnp.where(lane_half == 0, picked[0], picked[1]), picked[2]], axis=0)
    part[...] = tile
    parts[tensor] = tile
    for peer in tensor_peers:
        send(part, parts.at[tensor], sum_send, sum_recv, peer)

    up_o = weights(2)
    wait_bytes(parts.at[pl.ds(0, n_tensor - 1)], sum_recv)
    total = jnp.sum(parts[...], axis=0)
    rows = []
    for t in range(STEPS):
        tile = total[(t // 2) * ROWS : (t // 2 + 1) * ROWS]
        both = jnp.where(lane_half == t % 2, tile, pltpu.roll(tile, RANK, 1))
        rows.append(jnp.where(lane_half == half_of[t], both, 0.0))
    result = nn(jnp.concatenate(rows, axis=0).astype(BF16), up_o)
    for t in range(STEPS):
        adapter_out[t] = result[t * ROWS : (t + 1) * ROWS].astype(BF16)

    for p in range(2):
        wait_bytes(landed.at[p, pl.ds(0, GROUP - 1)], s1_send.at[p])
    wait_bytes(hid_own.at[pl.ds(0, n_block - 1)], hid_send)
    for m in range(3):
        wait_bytes(w_new.at[m, pl.ds(0, (n_block - 1) * GROUP)], s2_send.at[m])
    wait_bytes(rank_parts.at[pl.ds(0, n_block * n_tensor - 1)], rank_send)
    wait_bytes(parts.at[pl.ds(0, n_tensor - 1)], sum_send)


def body(
    n_replica, n_tensor,
    hidden_in, frozen_query_rows, base_key_value, cache, lengths, switch_step,
    old_down_q, current_query_up, old_down_o, old_up_o,
    new_down_q, refreshed_query_up, new_down_o, new_up_o,
):
    width = frozen_query_rows.shape[-1]
    cache_len = cache.shape[2]
    key_rows = cache_len + LANES
    tiles = width // LANES
    n_block = n_replica // GROUP
    dma = pltpu.SemaphoreType.DMA
    out = pltpu.VMEM(frozen_query_rows.shape, BF16)
    return pl.pallas_call(
        functools.partial(kernel, n_block, n_tensor, width, cache_len, key_rows),
        out_shape=(out, out),
        in_specs=[pl.BlockSpec(memory_space=pltpu.SMEM)]
        + [pl.BlockSpec(memory_space=pltpu.HBM)] * 13,
        out_specs=(pl.BlockSpec(memory_space=pltpu.VMEM),) * 2,
        scratch_shapes=[
            pltpu.VMEM(new_down_q.shape, BF16),
            pltpu.VMEM(refreshed_query_up.shape, BF16),
            pltpu.VMEM(new_down_o.shape, BF16),
            pltpu.VMEM(new_up_o.shape, BF16),
            pltpu.VMEM((n_block, STEPS, ROWS, width), BF16),
            pltpu.VMEM((n_block * STEPS * ROWS, width), BF16),
            pltpu.VMEM(hidden_in.shape, BF16),
            pltpu.VMEM(old_down_q.shape, BF16),
            pltpu.VMEM((STEPS, ROWS, width), BF16),
            pltpu.VMEM(base_key_value.shape, BF16),
            pltpu.VMEM((ROWS, key_rows, HD), BF16),
            pltpu.VMEM((ROWS, key_rows, HD), BF16),
            pltpu.VMEM((3, RANK, width), BF16),
            pltpu.VMEM((3, RANK, width), BF16),
            pltpu.VMEM((2, 2 * tiles, LANES), BF16),
            pltpu.VMEM((2, GROUP, 2 * tiles, LANES), BF16),
            pltpu.VMEM((2, 2 * tiles, LANES), F32),
            pltpu.VMEM((2, GROUP * 2 * tiles, LANES), F32),
            pltpu.VMEM((2, ROWS * ROWS, HD), F32),
            pltpu.VMEM((STEPS * ROWS, LANES), F32),
            pltpu.VMEM((STEPS, width // HD * ROWS, HD), F32),
            pltpu.VMEM((STEPS, width // HD * ROWS, HD), F32),
            pltpu.VMEM((n_block, ROWS, LANES), F32),
            pltpu.VMEM((n_block * n_tensor, ROWS, LANES), F32),
            pltpu.VMEM((2 * ROWS, LANES), F32),
            pltpu.VMEM((n_tensor, 2 * ROWS, LANES), F32),
            pltpu.SMEM(lengths.shape, jnp.int32),
            dma((13,)),
            dma((2, ROWS)),
            dma((2,)),
            dma((2,)),
            dma(()),
            dma(()),
            dma((3,)),
            dma((3,)),
            dma(()),
            dma(()),
            dma(()),
            dma(()),
        ],
        compiler_params=pltpu.CompilerParams(
            collective_id=0, has_side_effects=True, vmem_limit_bytes=32 * 1024 * 1024
        ),
    )(
        switch_step,
        *[
            pltpu.with_memory_space_constraint(operand, pltpu.HBM)
            for operand in (
                lengths, hidden_in, frozen_query_rows, base_key_value, cache,
                old_down_q, current_query_up, old_down_o, old_up_o,
                new_down_q, refreshed_query_up, new_down_o, new_up_o,
            )
        ],
    )


def solution(mesh):
    placed = (
        P(None, "replica", None),
        P(None, "replica", "tensor"),
        P(None, None, "replica", "tensor"),
        P(None, "replica", None, "tensor"),
        P("replica"),
        P("replica"),
        P(),
        P(None, "tensor"),
        P(None, "tensor"),
        P(),
        P("replica", None),
        P("replica", "tensor"),
        P("replica", "tensor"),
        P("replica", None),
    )
    return jax.shard_map(
        functools.partial(body, mesh.shape["replica"], mesh.shape["tensor"]),
        mesh=mesh,
        in_specs=placed,
        out_specs=(P(None, "replica", "tensor"), P(None, "replica", "tensor")),
        check_vma=False,
    )
```

time: 42.4 us -> 39.7 us (0.936)
  Pallas kernels: 39.6 us -> 37 us
    pallas_call x1, Pallas kernels: 39.6 us -> 37 us  [body(): pl.pallas_call(functools.partial(kernel, n_block, n_tensor, width, cache_...]
where the time goes in v4:
time: 39.7 us; the launch traced here: 39.6 us
  Pallas kernels  37 us (93%)
  between operations  1.29 us (3%)
  local copies, waits for them, and re-layouts  1.24 us (3%)
    pallas_call x1, Pallas kernels, body(): pl.pallas_call(functools.partial(kernel, n_block, n_tensor, width, cache_...  37 us
    unnamed x2, local copies, waits for them, and re-layouts  1.24 us

profile of v4, /device:TPU:1, one launch (start us, length us, event | category | flops | bytes accessed | tf_op | source)
XLA Modules:
  0.0 39.6 jit_solution(8362548025716388794)
XLA Ops:
  1.3 37.0 %shard_map.149 = (bf16[3,8,1024]{2,1,0:T(8,128)(2,1)S(1)}, bf16[3,8,1024]{2,1,0:T(8,128)(2,1)S(1)}) custom-call(s32[1]{0:T(128)S(6)} %copy.20.switch, s32[8]{0:T(128)} %lengths_in.1, bf16[3,8,8192]{2,1,0:T(8,128)(2,1)} %hidden.1, bf16[3,8,1024]{2,1,0:T(8,128)(2,1)} %frozen.1, bf16[2,3,8,128]{3,2,1,0:T(8,128)(2,1)} %fresh.1, bf16[2,8,384,128]{3,2,1,0:T(8,128)(2,1)} %cache.1, ...), custom_call_target="tpu_custom_call" | custom-call | tf_op jit(solution)/shard_map/pallas_call | solution.py:307
  38.3 0.6 %copy.18 = bf16[3,8,1024]{2,1,0:T(8,128)(2,1)} copy(bf16[3,8,1024]{2,1,0:T(8,128)(2,1)S(1)} %get-tuple-element.2) | data formatting | bytes 98304
  38.9 0.6 %copy.19 = bf16[3,8,1024]{2,1,0:T(8,128)(2,1)} copy(bf16[3,8,1024]{2,1,0:T(8,128)(2,1)S(1)} %get-tuple-element.3) | data formatting | bytes 98304

commit v5 on v4

--- a/solution.py
+++ b/solution.py
@@ -66,11 +66,6 @@
         for j in tensor_order
         if i or j
     ]
-    barrier = pltpu.get_barrier_semaphore()
-    everyone = group_peers + [peer for _, peer in rank_peers]
-    for peer in everyone:
-        pl.semaphore_signal(barrier, inc=1, device_id=peer, device_id_type=MESH)
-
     def send(src, dst, send_sem, recv_sem, peer):
         pltpu.make_async_remote_copy(
             src_ref=src,
@@ -101,28 +96,35 @@
     ]
     for copy in local[:5]:
         copy.start()
+    barrier = pltpu.get_barrier_semaphore()
+    everyone = group_peers + block_peers + tensor_peers
+    for peer in everyone:
+        pl.semaphore_signal(barrier, inc=1, device_id=peer, device_id_type=MESH)
     kv = []
     for b in range(ROWS):
         kv.append(pltpu.make_async_copy(cache.at[0, b], kbuf.at[b, pl.ds(0, cache_len)], kv_sem.at[0, b]))
         kv.append(pltpu.make_async_copy(cache.at[1, b], vbuf.at[b, pl.ds(0, cache_len)], kv_sem.at[1, b]))
 
-    for copy in local[:4]:
-        copy.wait()
-    for i, row in enumerate((row_dq[:, cols], row_uq[...], row_do[...], row_uo[:, cols])):
-        row = row.astype(F32)
-        for s in range(tiles):
-            stage[i // 2, pl.ds((i % 2) * tiles + s, 1), :] = row[:, s * LANES : (s + 1) * LANES]
-    for p in range(2):
+    def pack(p, rows):
+        for i, row in enumerate(rows):
+            row = row.astype(F32)
+            for c in range(tiles):
+                stage[p, pl.ds(i * tiles + c, 1), :] = row[:, c * LANES : (c + 1) * LANES]
         packs[p] = stage[p].astype(BF16)
         landed[p, mine] = packs[p]
 
+    for copy in local[:2]:
+        copy.wait()
+    pack(0, (row_dq[:, cols], row_uq[...]))
     pl.semaphore_wait(barrier, len(everyone))
-
     for peer in group_peers:
         send(packs.at[0], landed.at[0, mine], s1_send.at[0], s1_recv.at[0], peer)
     local[4].wait()
     for peer in block_peers:
         send(hid_own.at[block], hid_own.at[block], hid_send, hid_recv, peer)
+    for copy in local[2:4]:
+        copy.wait()
+    pack(1, (row_do[...], row_uo[:, cols]))
     for peer in group_peers:
         send(packs.at[1], landed.at[1, mine], s1_send.at[1], s1_recv.at[1], peer)
 
@@ -173,6 +175,16 @@
         wait_bytes(w_new.at[m, pl.ds(0, (n_block - 1) * GROUP)], s2_recv.at[m])
         return jnp.concatenate([w_old[m], w_new[m]], axis=0)
 
+    local[6].wait()
+    local[7].wait()
+    old_rank[...] = jnp.zeros_like(old_rank)
+    old = jnp.zeros((STEPS * ROWS, RANK), F32)
+    for c in range(n_tensor):
+        at = slice(c * width, (c + 1) * width)
+        rows = jnp.concatenate([hid_full[t, :, at].astype(F32) for t in range(STEPS)], axis=0)
+        old = old + nt(rows.astype(BF16), dq_full[:, at])
+    old_rank[:, 0:RANK] = old
+
     arrived(0)
     down_q = jnp.concatenate(rows_of(0), axis=1)
     ranks = nt(hid_rows[...], jnp.concatenate([down_q] * (LANES // GROUP), axis=0))
@@ -192,16 +204,6 @@
     share(1)
     share(2)
 
-    local[6].wait()
-    local[7].wait()
-    old_rank[...] = jnp.zeros_like(old_rank)
-    old = jnp.zeros((STEPS * ROWS, RANK), F32)
-    for c in range(n_tensor):
-        at = slice(c * width, (c + 1) * width)
-        rows = jnp.concatenate([hid_full[t, :, at].astype(F32) for t in range(STEPS)], axis=0)
-        old = old + nt(rows.astype(BF16), dq_full[:, at])
-    old_rank[:, 0:RANK] = old
-
     switch_at = jnp.full((ROWS, LANES), switch[0], jnp.int32)
     half_of = [jnp.where(switch_at <= t, 1, 0) for t in range(STEPS)]
 
@@ -236,18 +238,21 @@
     col = lax.broadcasted_iota(jnp.int32, (query_rows, key_rows), 1)
     row = lax.broadcasted_iota(jnp.int32, (query_rows, key_rows), 0)
     is_fresh = jnp.logical_and(col >= cache_len, (col - cache_len) * heads <= row)
+    queries = [
+        jnp.concatenate([q_heads[t, pl.ds(b, heads, stride=ROWS), :] for t in range(STEPS)], axis=0).astype(BF16)
+        for b in range(ROWS)
+    ]
+    scores = [nt(queries[b], kbuf[b]) for b in range(ROWS)]
+    probs = []
     for b in range(ROWS):
-        query = jnp.concatenate(
-            [q_heads[t, pl.ds(b, heads, stride=ROWS), :] for t in range(STEPS)], axis=0
-        ).astype(BF16)
-        scores = nt(query, kbuf[b]) * scale
         live = jnp.logical_or(col < lengths[b], is_fresh)
-        scores = jnp.where(live, scores, -1e30)
-        top = jnp.max(scores, axis=1, keepdims=True)
-        exps = jnp.exp(scores - top)
+        shown = jnp.where(live, scores[b] * scale, -1e30)
+        top = jnp.max(shown, axis=1, keepdims=True)
+        exps = jnp.exp(shown - top)
         total = jnp.sum(exps, axis=1, keepdims=True)
-        probs = (exps * (1.0 / total)).astype(BF16)
-        result = nn(probs, vbuf[b])
+        probs.append((exps * (1.0 / total)).astype(BF16))
+    for b in range(ROWS):
+        result = nn(probs[b], vbuf[b])
         for t in range(STEPS):
             a_rows[t, pl.ds(b * heads, heads), :] = result[t * heads : (t + 1) * heads]
 
@@ -289,6 +294,17 @@
         wait_bytes(w_new.at[m, pl.ds(0, (n_block - 1) * GROUP)], s2_send.at[m])
     wait_bytes(rank_parts.at[pl.ds(0, n_block * n_tensor - 1)], rank_send)
     wait_bytes(parts.at[pl.ds(0, n_tensor - 1)], sum_send)
+
+
+def write_out(attended, adapter, attended_out, adapter_out, sems):
+    copies = [
+        pltpu.make_async_copy(attended, attended_out, sems.at[0]),
+        pltpu.make_async_copy(adapter, adapter_out, sems.at[1]),
+    ]
+    for copy in copies:
+        copy.start()
+    for copy in copies:
+        copy.wait()
 
 
 def body(
@@ -304,7 +320,7 @@
     n_block = n_replica // GROUP
     dma = pltpu.SemaphoreType.DMA
     out = pltpu.VMEM(frozen_query_rows.shape, BF16)
-    return pl.pallas_call(
+    results = pl.pallas_call(
         functools.partial(kernel, n_block, n_tensor, width, cache_len, key_rows),
         out_shape=(out, out),
         in_specs=[pl.BlockSpec(memory_space=pltpu.SMEM)]
@@ -365,6 +381,14 @@
             )
         ],
     )
+    written = jax.ShapeDtypeStruct(frozen_query_rows.shape, BF16)
+    return pl.pallas_call(
+        write_out,
+        out_shape=(written, written),
+        in_specs=[pl.BlockSpec(memory_space=pltpu.VMEM)] * 2,
+        out_specs=(pl.BlockSpec(memory_space=pl.ANY),) * 2,
+        scratch_shapes=[dma((2,))],
+    )(*[pltpu.with_memory_space_constraint(result, pltpu.VMEM) for result in results])
 
 
 def solution(mesh):

time: 39.7 us -> 36.2 us (0.912)
  Pallas kernels: 37 us -> 34.8 us
  local copies, waits for them, and re-layouts: 1.24 us -> 0 us
    pallas_call x1, Pallas kernels: 37 us -> 34.1 us  [body(): pl.pallas_call(functools.partial(kernel, n_block, n_tensor, width, cache_...]
    unnamed x2 -> x0, local copies, waits for them, and re-layouts: 1.24 us -> none
    pallas_call x0 -> x1, Pallas kernels: none -> 0.66 us  [body(): pl.pallas_call(write_out, out_shape=(written, written), in_specs=[pl.Bloc...]
where the time goes in v5:
time: 36.2 us; the launch traced here: 36 us
  Pallas kernels  34.8 us (96%)
  between operations  1.29 us (4%)
    pallas_call x1, Pallas kernels, body(): pl.pallas_call(functools.partial(kernel, n_block, n_tensor, width, cache_...  34.1 us

profile of v5, /device:TPU:1, one launch (start us, length us, event | category | flops | bytes accessed | tf_op | source)
XLA Modules:
  0.0 36.0 jit_solution(4770086230178614647)
XLA Ops:
  1.3 34.1 %shard_map.149 = (bf16[3,8,1024]{2,1,0:T(8,128)(2,1)S(1)}, bf16[3,8,1024]{2,1,0:T(8,128)(2,1)S(1)}) custom-call(s32[1]{0:T(128)S(6)} %copy.16.switch, s32[8]{0:T(128)} %lengths_in.1, bf16[3,8,8192]{2,1,0:T(8,128)(2,1)} %hidden.1, bf16[3,8,1024]{2,1,0:T(8,128)(2,1)} %frozen.1, bf16[2,3,8,128]{3,2,1,0:T(8,128)(2,1)} %fresh.1, bf16[2,8,384,128]{3,2,1,0:T(8,128)(2,1)} %cache.1, ...), custom_call_target="tpu_custom_call" | custom-call | tf_op jit(solution)/shard_map/pallas_call | solution.py:323
  35.4 0.7 %shard_map.150 = (bf16[3,8,1024]{2,1,0:T(8,128)(2,1)}, bf16[3,8,1024]{2,1,0:T(8,128)(2,1)}) custom-call(bf16[3,8,1024]{2,1,0:T(8,128)(2,1)S(1)} %get-tuple-element.4.attended, bf16[3,8,1024]{2,1,0:T(8,128)(2,1)S(1)} %get-tuple-element.5.adapter), custom_call_target="tpu_custom_call" | custom-call | tf_op jit(solution)/shard_map/pallas_call | solution.py:385

commit v6 on v5

--- a/solution.py
+++ b/solution.py
@@ -13,6 +13,8 @@
 RANK = 64
 GROUP = 16
 LANES = 128
+HALF = ROWS // 2
+SHARES = 4
 MESH = pl.DeviceIdType.MESH
 F32 = jnp.float32
 BF16 = jnp.bfloat16
@@ -32,9 +34,9 @@
     old_dq, old_uq, old_do, old_uo, new_dq, new_uq, new_do, new_uo,
     attended_out, adapter_out,
     row_dq, row_uq, row_do, row_uo, hid_own, hid_rows, hid_full, dq_full, frz, frs, kbuf, vbuf,
-    w_old, w_new, packs, landed, stage, spread, fresh_rows, old_rank, q_heads, a_rows,
+    w_old, w_new, pack_q, landed_q, stage_q, spread_q, packs, landed, stage, spread, fresh_rows, old_rank, q_heads, a_rows,
     rank_part, rank_parts, part, parts, lengths,
-    loc, kv_sem, s1_send, s1_recv, hid_send, hid_recv, s2_send, s2_recv,
+    others_in, loc, kv_sem, q_send, q_recv, s1_send, s1_recv, hid_send, hid_recv, s2_send, s2_recv,
     rank_send, rank_recv, sum_send, sum_recv,
 ):
     replica = lax.axis_index("replica")
@@ -43,6 +45,12 @@
     block = lax.div(replica, GROUP)
     base = block * GROUP
     cols = pl.ds(pl.multiple_of(tensor * width, width), width)
+    leads = tensor < SHARES
+    share_width = n_tensor // SHARES * width
+    rank_cols = pl.ds(
+        pl.multiple_of(lax.rem(tensor, SHARES) * share_width, share_width), share_width
+    )
+    rank_tiles = share_width // LANES
     heads = width // HD
     tiles = width // LANES
 
@@ -84,7 +92,7 @@
         pltpu.make_async_copy(new_uq, row_uq, loc.at[1]),
         pltpu.make_async_copy(new_do, row_do, loc.at[2]),
         pltpu.make_async_copy(new_uo, row_uo, loc.at[3]),
-        pltpu.make_async_copy(hidden.at[:, :, cols], hid_own.at[block], loc.at[4]),
+        pltpu.make_async_copy(hidden.at[:, :, rank_cols], hid_own.at[block], loc.at[4]),
         pltpu.make_async_copy(fresh, frs, loc.at[5]),
         pltpu.make_async_copy(hidden, hid_full, loc.at[6]),
         pltpu.make_async_copy(old_dq, dq_full, loc.at[7]),
@@ -97,36 +105,83 @@
     for copy in local[:5]:
         copy.start()
     barrier = pltpu.get_barrier_semaphore()
-    everyone = group_peers + block_peers + tensor_peers
-    for peer in everyone:
-        pl.semaphore_signal(barrier, inc=1, device_id=peer, device_id_type=MESH)
+    own_half = lax.div(tensor, SHARES) * SHARES
+    half_peers = [
+        (replica, own_half + lax.rem(tensor + j, SHARES)) for j in range(1, SHARES)
+    ]
+    close = group_peers + block_peers + half_peers
+    across = [
+        (block_at(i) * GROUP + mine, SHARES - own_half + j)
+        for i in block_order
+        for j in range(SHARES)
+    ]
+
+    def signal(semaphore, peers):
+        for peer in peers:
+            pl.semaphore_signal(semaphore, inc=1, device_id=peer, device_id_type=MESH)
+
+    signal(barrier, close)
+
+    @pl.when(leads)
+    def _():
+        signal(barrier, across)
+
     kv = []
     for b in range(ROWS):
         kv.append(pltpu.make_async_copy(cache.at[0, b], kbuf.at[b, pl.ds(0, cache_len)], kv_sem.at[0, b]))
         kv.append(pltpu.make_async_copy(cache.at[1, b], vbuf.at[b, pl.ds(0, cache_len)], kv_sem.at[1, b]))
 
-    def pack(p, rows):
-        for i, row in enumerate(rows):
+    def tiled(buf, rows):
+        at = 0
+        for row in rows:
             row = row.astype(F32)
-            for c in range(tiles):
-                stage[p, pl.ds(i * tiles + c, 1), :] = row[:, c * LANES : (c + 1) * LANES]
+            for c in range(row.shape[1] // LANES):
+                buf[pl.ds(at + c, 1), :] = row[:, c * LANES : (c + 1) * LANES]
+            at += row.shape[1] // LANES
+
+    local[0].wait()
+
+    @pl.when(leads)
+    def _():
+        tiled(stage_q, [row_dq[:, rank_cols]])
+        pack_q[...] = stage_q[...].astype(BF16)
+        landed_q[mine] = pack_q[...]
+
+    @pl.when(leads)
+    def _():
+        pl.semaphore_wait(barrier, len(close))
+
+    @pl.when(jnp.logical_not(leads))
+    def _():
+        pl.semaphore_wait(barrier, len(close) + len(across))
+        signal(others_in, across)
+
+
+    local[4].wait()
+
+    @pl.when(leads)
+    def _():
+        for peer in block_peers:
+            send(hid_own.at[block], hid_own.at[block], hid_send, hid_recv, peer)
+
+    @pl.when(leads)
+    def _():
+        for peer in group_peers:
+            send(pack_q, landed_q.at[mine], q_send, q_recv, peer)
+
+    def spread_rows(p, rows):
+        tiled(stage.at[p], rows)
         packs[p] = stage[p].astype(BF16)
         landed[p, mine] = packs[p]
-
-    for copy in local[:2]:
+        for peer in group_peers:
+            send(packs.at[p], landed.at[p, mine], s1_send.at[p], s1_recv.at[p], peer)
+
+    for copy in local[1:3]:
         copy.wait()
-    pack(0, (row_dq[:, cols], row_uq[...]))
-    pl.semaphore_wait(barrier, len(everyone))
-    for peer in group_peers:
-        send(packs.at[0], landed.at[0, mine], s1_send.at[0], s1_recv.at[0], peer)
-    local[4].wait()
-    for peer in block_peers:
-        send(hid_own.at[block], hid_own.at[block], hid_send, hid_recv, peer)
-    for copy in local[2:4]:
-        copy.wait()
-    pack(1, (row_do[...], row_uo[:, cols]))
-    for peer in group_peers:
-        send(packs.at[1], landed.at[1, mine], s1_send.at[1], s1_recv.at[1], peer)
+    spread_rows(0, [row_uq[...], row_do[...]])
+
+    local[3].wait()
+    spread_rows(1, [row_uo[:, cols], jnp.zeros((1, width), F32)])
 
     for copy in local[5:] + kv:
         copy.start()
@@ -145,36 +200,6 @@
             buf[b, pl.ds(cache_len, 16), :] = rows.astype(BF16)
             buf[b, pl.ds(cache_len + 16, pad), :] = jnp.zeros((pad, HD), BF16)
 
-    wait_bytes(hid_own.at[pl.ds(0, n_block - 1)], hid_recv)
-    for k in range(n_block):
-        rows = jnp.concatenate([hid_own[k, t].astype(F32) for t in range(STEPS)], axis=0)
-        hid_rows[pl.ds(k * STEPS * ROWS, STEPS * ROWS), :] = rows.astype(BF16)
-
-    own_rows = pl.ds(pl.multiple_of(block * GROUP, GROUP), GROUP)
-    lane = lax.broadcasted_iota(jnp.int32, (ROWS, LANES), 1)
-    lane_half = lax.div(lane, RANK)
-    lane_group = lax.div(lane, GROUP)
-
-    def arrived(p):
-        wait_bytes(landed.at[p, pl.ds(0, GROUP - 1)], s1_recv.at[p])
-        spread[p] = landed[p].reshape(GROUP * 2 * tiles, LANES).astype(F32)
-
-    def rows_of(i):
-        return [
-            spread[i // 2, pl.ds((i % 2) * tiles + s, GROUP, stride=2 * tiles), :].astype(BF16)
-            for s in range(tiles)
-        ]
-
-    def share(m):
-        for s, tile in enumerate(rows_of(m + 1)):
-            w_new[m, own_rows, s * LANES : (s + 1) * LANES] = tile
-        for peer in block_peers:
-            send(w_new.at[m, own_rows], w_new.at[m, own_rows], s2_send.at[m], s2_recv.at[m], peer)
-
-    def weights(m):
-        wait_bytes(w_new.at[m, pl.ds(0, (n_block - 1) * GROUP)], s2_recv.at[m])
-        return jnp.concatenate([w_old[m], w_new[m]], axis=0)
-
     local[6].wait()
     local[7].wait()
     old_rank[...] = jnp.zeros_like(old_rank)
@@ -185,23 +210,63 @@
         old = old + nt(rows.astype(BF16), dq_full[:, at])
     old_rank[:, 0:RANK] = old
 
+    own_rows = pl.ds(pl.multiple_of(block * GROUP, GROUP), GROUP)
+    lane = lax.broadcasted_iota(jnp.int32, (ROWS, LANES), 1)
+    lane_half = lax.div(lane, RANK)
+    lane_group = lax.div(lane, GROUP)
+
+    def arrived(p):
+        wait_bytes(landed.at[p, pl.ds(0, GROUP - 1)], s1_recv.at[p])
+        spread[p] = landed[p].reshape(GROUP * 2 * tiles, LANES).astype(F32)
+
+    def rows_of(i):
+        return [
+            spread[i // 2, pl.ds((i % 2) * tiles + s, GROUP, stride=2 * tiles), :].astype(BF16)
+            for s in range(tiles)
+        ]
+
+    def share(m):
+        for s, tile in enumerate(rows_of(m)):
+            w_new[m, own_rows, s * LANES : (s + 1) * LANES] = tile
+        for peer in block_peers:
+            send(w_new.at[m, own_rows], w_new.at[m, own_rows], s2_send.at[m], s2_recv.at[m], peer)
+
+    def weights(m):
+        wait_bytes(w_new.at[m, pl.ds(0, (n_block - 1) * GROUP)], s2_recv.at[m])
+        return jnp.concatenate([w_old[m], w_new[m]], axis=0)
+
+    @pl.when(leads)
+    def _():
+        wait_bytes(hid_own.at[pl.ds(0, n_block - 1)], hid_recv)
+        for k in range(n_block):
+            rows = jnp.concatenate([hid_own[k, t].astype(F32) for t in range(STEPS)], axis=0)
+            hid_rows[pl.ds(k * STEPS * ROWS, STEPS * ROWS), :] = rows.astype(BF16)
+        wait_bytes(landed_q.at[pl.ds(0, GROUP - 1)], q_recv)
+        spread_q[...] = landed_q[...].reshape(GROUP * rank_tiles, LANES).astype(F32)
+        down_q = jnp.concatenate(
+            [
+                spread_q[pl.ds(c, GROUP, stride=rank_tiles), :].astype(BF16)
+                for c in range(rank_tiles)
+            ],
+            axis=1,
+        )
+        ranks = nt(hid_rows[...], jnp.concatenate([down_q] * (LANES // GROUP), axis=0))
+        for k in range(n_block):
+            tile = jnp.zeros((ROWS, LANES), F32)
+            for t in range(STEPS):
+                at = (k * STEPS + t) * ROWS
+                tile = jnp.where(lane_group == t, ranks[at : at + ROWS], tile)
+            rank_part[k] = tile[:HALF] + pltpu.roll(tile[HALF:], STEPS * GROUP, 1)
+        slot = block * SHARES + tensor
+        rank_parts[slot] = rank_part[block]
+        pl.semaphore_wait(others_in, len(across))
+        for k, peer in rank_peers:
+            send(rank_part.at[k], rank_parts.at[slot], rank_send, rank_recv, peer)
+
     arrived(0)
-    down_q = jnp.concatenate(rows_of(0), axis=1)
-    ranks = nt(hid_rows[...], jnp.concatenate([down_q] * (LANES // GROUP), axis=0))
-    for k in range(n_block):
-        tile = jnp.zeros((ROWS, LANES), F32)
-        for t in range(STEPS):
-            at = (k * STEPS + t) * ROWS
-            tile = jnp.where(lane_group == t, ranks[at : at + ROWS], tile)
-        rank_part[k] = tile
-    slot = block * n_tensor + tensor
-    rank_parts[slot] = rank_part[block]
-    for k, peer in rank_peers:
-        send(rank_part.at[k], rank_parts.at[slot], rank_send, rank_recv, peer)
-
     share(0)
+    share(1)
     arrived(1)
-    share(1)
     share(2)
 
     switch_at = jnp.full((ROWS, LANES), switch[0], jnp.int32)
@@ -212,10 +277,20 @@
     for copy in kv:
         copy.wait()
 
-    wait_bytes(rank_parts.at[pl.ds(0, n_block * n_tensor - 1)], rank_recv)
-    sums = [
-        jnp.sum(rank_parts[k * n_tensor : (k + 1) * n_tensor], axis=0) for k in range(n_block)
-    ]
+    @pl.when(leads)
+    def _():
+        wait_bytes(rank_parts.at[pl.ds(0, n_block * SHARES - 1)], rank_recv)
+
+    @pl.when(jnp.logical_not(leads))
+    def _():
+        wait_bytes(rank_parts.at[pl.ds(0, n_block * SHARES)], rank_recv)
+
+    sums = []
+    for k in range(n_block):
+        tile = jnp.sum(rank_parts[k * SHARES : (k + 1) * SHARES], axis=0)
+        sums.append(
+            jnp.concatenate([tile, pltpu.roll(tile, LANES - STEPS * GROUP, 1)], axis=0)
+        )
     chosen = []
     for t in range(STEPS):
         both = old_rank[t * ROWS : (t + 1) * ROWS]
@@ -269,30 +344,46 @@
     for t in range(STEPS):
         rows = product[t * ROWS : (t + 1) * ROWS]
         picked.append(jnp.where(half_of[t] == t % 2, rows, pltpu.roll(rows, RANK, 1)))
-    tile = jnp.concatenate([jnp.where(lane_half == 0, picked[0], picked[1]), picked[2]], axis=0)
-    part[...] = tile
-    parts[tensor] = tile
+    tile = jnp.where(lane_half == 0, picked[0], picked[1])
+    last = jnp.where(
+        lane_half[:HALF] == 0, picked[2][:HALF], pltpu.roll(picked[2][HALF:], RANK, 1)
+    )
+    for i, piece in enumerate((tile[:HALF], tile[HALF:], last)):
+        part[i] = piece
+        parts[tensor, i] = piece
     for peer in tensor_peers:
         send(part, parts.at[tensor], sum_send, sum_recv, peer)
 
     up_o = weights(2)
     wait_bytes(parts.at[pl.ds(0, n_tensor - 1)], sum_recv)
     total = jnp.sum(parts[...], axis=0)
-    rows = []
-    for t in range(STEPS):
-        tile = total[(t // 2) * ROWS : (t // 2 + 1) * ROWS]
-        both = jnp.where(lane_half == t % 2, tile, pltpu.roll(tile, RANK, 1))
-        rows.append(jnp.where(lane_half == half_of[t], both, 0.0))
+    tile = jnp.concatenate([total[0], total[1]], axis=0)
+    other = pltpu.roll(tile, RANK, 1)
+    last = jnp.concatenate([total[2], total[2]], axis=0)
+    last_other = pltpu.roll(last, RANK, 1)
+    row_half = lax.div(lax.broadcasted_iota(jnp.int32, (ROWS, LANES), 0), HALF)
+    both = (
+        jnp.where(lane_half == 0, tile, other),
+        jnp.where(lane_half == 1, tile, other),
+        jnp.where(lane_half == row_half, last, last_other),
+    )
+    rows = [jnp.where(lane_half == half_of[t], both[t], 0.0) for t in range(STEPS)]
     result = nn(jnp.concatenate(rows, axis=0).astype(BF16), up_o)
     for t in range(STEPS):
         adapter_out[t] = result[t * ROWS : (t + 1) * ROWS].astype(BF16)
 
     for p in range(2):
         wait_bytes(landed.at[p, pl.ds(0, GROUP - 1)], s1_send.at[p])
-    wait_bytes(hid_own.at[pl.ds(0, n_block - 1)], hid_send)
     for m in range(3):
         wait_bytes(w_new.at[m, pl.ds(0, (n_block - 1) * GROUP)], s2_send.at[m])
-    wait_bytes(rank_parts.at[pl.ds(0, n_block * n_tensor - 1)], rank_send)
+
+    @pl.when(leads)
+    def _():
+        wait_bytes(landed_q.at[pl.ds(0, GROUP - 1)], q_send)
+        wait_bytes(hid_own.at[pl.ds(0, n_block - 1)], hid_send)
+        wait_bytes(rank_parts.at[pl.ds(0, n_block * SHARES)], rank_send)
+        wait_bytes(rank_parts.at[pl.ds(0, n_block * SHARES - 1)], rank_send)
+
     wait_bytes(parts.at[pl.ds(0, n_tensor - 1)], sum_send)
 
 
@@ -318,6 +409,8 @@
     key_rows = cache_len + LANES
     tiles = width // LANES
     n_block = n_replica // GROUP
+    share_width = n_tensor // SHARES * width
+    rank_tiles = share_width // LANES
     dma = pltpu.SemaphoreType.DMA
     out = pltpu.VMEM(frozen_query_rows.shape, BF16)
     results = pl.pallas_call(
@@ -331,8 +424,8 @@
             pltpu.VMEM(refreshed_query_up.shape, BF16),
             pltpu.VMEM(new_down_o.shape, BF16),
             pltpu.VMEM(new_up_o.shape, BF16),
-            pltpu.VMEM((n_block, STEPS, ROWS, width), BF16),
-            pltpu.VMEM((n_block * STEPS * ROWS, width), BF16),
+            pltpu.VMEM((n_block, STEPS, ROWS, share_width), BF16),
+            pltpu.VMEM((n_block * STEPS * ROWS, share_width), BF16),
             pltpu.VMEM(hidden_in.shape, BF16),
             pltpu.VMEM(old_down_q.shape, BF16),
             pltpu.VMEM((STEPS, ROWS, width), BF16),
@@ -341,6 +434,10 @@
             pltpu.VMEM((ROWS, key_rows, HD), BF16),
             pltpu.VMEM((3, RANK, width), BF16),
             pltpu.VMEM((3, RANK, width), BF16),
+            pltpu.VMEM((rank_tiles, LANES), BF16),
+            pltpu.VMEM((GROUP, rank_tiles, LANES), BF16),
+            pltpu.VMEM((rank_tiles, LANES), F32),
+            pltpu.VMEM((GROUP * rank_tiles, LANES), F32),
             pltpu.VMEM((2, 2 * tiles, LANES), BF16),
             pltpu.VMEM((2, GROUP, 2 * tiles, LANES), BF16),
             pltpu.VMEM((2, 2 * tiles, LANES), F32),
@@ -349,13 +446,16 @@
             pltpu.VMEM((STEPS * ROWS, LANES), F32),
             pltpu.VMEM((STEPS, width // HD * ROWS, HD), F32),
             pltpu.VMEM((STEPS, width // HD * ROWS, HD), F32),
-            pltpu.VMEM((n_block, ROWS, LANES), F32),
-            pltpu.VMEM((n_block * n_tensor, ROWS, LANES), F32),
-            pltpu.VMEM((2 * ROWS, LANES), F32),
-            pltpu.VMEM((n_tensor, 2 * ROWS, LANES), F32),
+            pltpu.VMEM((n_block, HALF, LANES), F32),
+            pltpu.VMEM((n_block * SHARES, HALF, LANES), F32),
+            pltpu.VMEM((STEPS, HALF, LANES), F32),
+            pltpu.VMEM((n_tensor, STEPS, HALF, LANES), F32),
             pltpu.SMEM(lengths.shape, jnp.int32),
+            pltpu.SemaphoreType.REGULAR,
             dma((13,)),
             dma((2, ROWS)),
+            dma(()),
+            dma(()),
             dma((2,)),
             dma((2,)),
             dma(()),

time: 36.2 us -> 34.5 us (0.953)
  Pallas kernels: 34.8 us -> 33 us
    pallas_call x1, Pallas kernels: 34.1 us -> 32.4 us  [body(): pl.pallas_call(functools.partial(kernel, n_block, n_tensor, width, cache_...]
where the time goes in v6:
time: 34.5 us; the launch traced here: 34.3 us
  Pallas kernels  33 us (96%)
  between operations  1.29 us (4%)
    pallas_call x1, Pallas kernels, body(): pl.pallas_call(functools.partial(kernel, n_block, n_tensor, width, cache_...  32.4 us

profile of v6, /device:TPU:1, one launch (start us, length us, event | category | flops | bytes accessed | tf_op | source)
XLA Modules:
  0.0 34.3 jit_solution(13549275081299823438)
XLA Ops:
  1.3 32.4 %shard_map.149 = (bf16[3,8,1024]{2,1,0:T(8,128)(2,1)S(1)}, bf16[3,8,1024]{2,1,0:T(8,128)(2,1)S(1)}) custom-call(s32[1]{0:T(128)S(6)} %copy.16.switch, s32[8]{0:T(128)} %lengths_in.1, bf16[3,8,8192]{2,1,0:T(8,128)(2,1)} %hidden.1, bf16[3,8,1024]{2,1,0:T(8,128)(2,1)} %frozen.1, bf16[2,3,8,128]{3,2,1,0:T(8,128)(2,1)} %fresh.1, bf16[2,8,384,128]{3,2,1,0:T(8,128)(2,1)} %cache.1, ...), custom_call_target="tpu_custom_call" | custom-call | tf_op jit(solution)/shard_map/pallas_call | solution.py:416
  33.7 0.7 %shard_map.150 = (bf16[3,8,1024]{2,1,0:T(8,128)(2,1)}, bf16[3,8,1024]{2,1,0:T(8,128)(2,1)}) custom-call(bf16[3,8,1024]{2,1,0:T(8,128)(2,1)S(1)} %get-tuple-element.4.attended, bf16[3,8,1024]{2,1,0:T(8,128)(2,1)S(1)} %get-tuple-element.5.adapter), custom_call_target="tpu_custom_call" | custom-call | tf_op jit(solution)/shard_map/pallas_call | solution.py:485

commit v7 on v6

--- a/solution.py
+++ b/solution.py
@@ -102,8 +102,14 @@
         pltpu.make_async_copy(old_uo.at[:, cols], w_old.at[2], loc.at[11]),
         pltpu.make_async_copy(lengths_in, lengths, loc.at[12]),
     ]
-    for copy in local[:5]:
+    for copy in local[1:4]:
         copy.start()
+
+    @pl.when(leads)
+    def _():
+        local[0].start()
+        local[4].start()
+
     barrier = pltpu.get_barrier_semaphore()
     own_half = lax.div(tensor, SHARES) * SHARES
     half_peers = [
@@ -139,10 +145,9 @@
                 buf[pl.ds(at + c, 1), :] = row[:, c * LANES : (c + 1) * LANES]
             at += row.shape[1] // LANES
 
-    local[0].wait()
-
-    @pl.when(leads)
-    def _():
+    @pl.when(leads)
+    def _():
+        local[0].wait()
         tiled(stage_q, [row_dq[:, rank_cols]])
         pack_q[...] = stage_q[...].astype(BF16)
         landed_q[mine] = pack_q[...]
@@ -157,10 +162,9 @@
         signal(others_in, across)
 
 
-    local[4].wait()
-
-    @pl.when(leads)
-    def _():
+    @pl.when(leads)
+    def _():
+        local[4].wait()
         for peer in block_peers:
             send(hid_own.at[block], hid_own.at[block], hid_send, hid_recv, peer)
 
@@ -264,8 +268,8 @@
             send(rank_part.at[k], rank_parts.at[slot], rank_send, rank_recv, peer)
 
     arrived(0)
+    share(1)
     share(0)
-    share(1)
     arrived(1)
     share(2)
 

time: 34.5 us -> 34.5 us (level)
  no operation moved by 1% of the time
where the time goes in v7:
time: 34.5 us; the launch traced here: 34.3 us
  Pallas kernels  33 us (96%)
  between operations  1.29 us (4%)
    pallas_call x1, Pallas kernels, body(): pl.pallas_call(functools.partial(kernel, n_block, n_tensor, width, cache_...  32.4 us

profile of v7, /device:TPU:1, one launch (start us, length us, event | category | flops | bytes accessed | tf_op | source)
XLA Modules:
  0.0 34.3 jit_solution(5685401339979148237)
XLA Ops:
  1.3 32.4 %shard_map.149 = (bf16[3,8,1024]{2,1,0:T(8,128)(2,1)S(1)}, bf16[3,8,1024]{2,1,0:T(8,128)(2,1)S(1)}) custom-call(s32[1]{0:T(128)S(6)} %copy.16.switch, s32[8]{0:T(128)} %lengths_in.1, bf16[3,8,8192]{2,1,0:T(8,128)(2,1)} %hidden.1, bf16[3,8,1024]{2,1,0:T(8,128)(2,1)} %frozen.1, bf16[2,3,8,128]{3,2,1,0:T(8,128)(2,1)} %fresh.1, bf16[2,8,384,128]{3,2,1,0:T(8,128)(2,1)} %cache.1, ...), custom_call_target="tpu_custom_call" | custom-call | tf_op jit(solution)/shard_map/pallas_call | solution.py:420
  33.7 0.7 %shard_map.150 = (bf16[3,8,1024]{2,1,0:T(8,128)(2,1)}, bf16[3,8,1024]{2,1,0:T(8,128)(2,1)}) custom-call(bf16[3,8,1024]{2,1,0:T(8,128)(2,1)S(1)} %get-tuple-element.4.attended, bf16[3,8,1024]{2,1,0:T(8,128)(2,1)S(1)} %get-tuple-element.5.adapter), custom_call_target="tpu_custom_call" | custom-call | tf_op jit(solution)/shard_map/pallas_call | solution.py:489
